TPU v7x, 128 devices: a whole 4x4x4 slice. The times are simulated.
128 devices in a mesh: var: 32 (over y, z, core), mem: 4 (over x).
Axes of the slice: x: 4, y: 4, z: 4, core: 2. Of those that a mesh axis runs over, the one named last changes fastest.
Arguments:
- ensemble: float32 [80, 2097152], P('mem', 'var'), may hold values from -6 to 6
- ray_cells: int32 [4, 256, 64], replicated, may hold values from 0 to 2097151
- ray_weights: float32 [4, 256, 64], replicated, may hold values from 0.06 to 0.19
- ray_centers: int32 [4, 256], replicated, may hold values from 0 to 127
- obs_values: float32 [4, 256], replicated, may hold values from -6 to 6
- obs_var: float32 [4, 256], replicated, may hold values from 0.25 to 4
Outputs:
- posterior: float32 [80, 2097152], P('mem', 'var')
All inputs are finite; a program needn't handle non-finite values.
Results may differ from a plain program's by a relative error of at most 0.00014.
Values sent between devices are 32-bit elements; how exact they have to be, the bound alone decides.
A program may use at most 128 MiB of HBM per device.

v0:
```python
import jax
import jax.numpy as jnp
from jax import lax
from jax.sharding import PartitionSpec as P

CELLS = 16384
NBATCH = 4
LRAD = 4


HIGHEST_PREC = lax.Precision.HIGHEST
EPSILON = 1e-06


def innovations(prior_ens, obs_now, error_var):
    members = prior_ens.shape[0]
    prior_mean = jnp.mean(prior_ens, axis=0)
    anomaly = prior_ens - prior_mean
    variance = jnp.sum(anomaly * anomaly, axis=0) / (members - 1) + EPSILON
    total_var = variance + error_var
    post_mean = (prior_mean * error_var + obs_now * variance) / total_var
    shrink = jnp.sqrt(error_var / total_var)
    increments = post_mean - prior_mean + (shrink - 1.0) * anomaly
    regress = anomaly / ((members - 1) * variance)
    return (increments, regress)


def taper_weights(positions, centers):
    centre_pos = (centers.astype(jnp.float32) + 0.5) * CELLS
    distance = jnp.abs(positions[None, :] - centre_pos[:, None]) / (LRAD * CELLS)
    return jnp.maximum(0.0, 1.0 - distance)


def increment_block(cell_block, positions, increments, regress, centers):
    slopes = jnp.dot(regress.T, cell_block, precision=HIGHEST_PREC)
    slopes = slopes * taper_weights(positions, centers)
    return cell_block + jnp.dot(increments, slopes, precision=HIGHEST_PREC)


def shards(ensemble, ray_cells, ray_weights, ray_centers, obs_values, obs_var):
    groups = lax.axis_size("mem")
    cell_count = ensemble.shape[1] // groups
    anchor = (lax.axis_index("var") * groups + lax.axis_index("mem")) * cell_count
    positions = (anchor + jnp.arange(cell_count, dtype=jnp.int32)).astype(jnp.float32)
    columns = lax.all_to_all(ensemble, "mem", split_axis=1, concat_axis=0, tiled=True)
    for batch_index in range(NBATCH):
        offsets = ray_cells[batch_index] - anchor
        inside = (offsets >= 0) & (offsets < cell_count)
        clipped = jnp.clip(offsets, 0, cell_count - 1)
        picked = jnp.take(columns, clipped.reshape(-1), axis=1)
        picked = picked.reshape(columns.shape[0], clipped.shape[0], clipped.shape[1])
        weights_here = jnp.where(inside, ray_weights[batch_index], 0.0)
        partial_ens = jnp.einsum("mjk,jk->mj", picked, weights_here, precision=HIGHEST_PREC)
        prior_ens = lax.psum(partial_ens, ("var", "mem"))
        increments, regress = innovations(prior_ens, obs_values[batch_index], obs_var[batch_index])
        columns = increment_block(columns, positions, increments, regress, ray_centers[batch_index])
    ensemble = lax.all_to_all(columns, "mem", split_axis=0, concat_axis=1, tiled=True)
    return ensemble


def solution(mesh):
    placed = (P("mem", "var"), P(), P(), P(), P(), P())
    return jax.shard_map(
        shards, mesh=mesh, in_specs=placed, out_specs=P("mem", "var"), check_vma=False
    )
```

profile of v0, /device:TPU:1, one launch (start us, length us, event | category | flops | bytes accessed | tf_op | source)
XLA Modules:
  0.0 1190.1 jit_solution(3283146051670460788)
XLA Ops:
  6.5 7.1 all_to_all.28
  13.6 8.2 copy.32
  21.9 5.4 all-to-all-start
  28.5 69.9 %all-to-all-done = f32[20,4,16384]{2,0,1:T(8,128)} async-done(((f32[20,4,16384]{2,0,1:T(8,128)}), f32[20,4,16384]{2,0,1:T(8,128)}, u32[]{:S(2)}, u32[]{:S(2)}) %all-to-all-start) | async-done | bytes 5242912 | tf_op jit(solution)/shard_map/all_to_all | solution.py:45
  98.4 4.6 all_to_all.31
  103.0 7.9 copy.34
  111.0 58.2 %gather_fusion = f32[16384,80]{1,0:T(8,128)} fusion(f32[80,16384]{0,1:T(8,128)} %copy.34, s32[16384]{0:T(1024)S(1)} %fusion.24), kind=kCustom, calls=%fused_computation.clone | custom fusion | bytes 10551296 | tf_op jit(solution)/shard_map/jit(_take)/gather | solution.py:50
  169.2 6.9 multiply_reduce_fusion.3
  176.0 0.7 copy.46
  176.8 0.3 all-reduce.7.cloned.1.call-start
  177.2 139.8 %all-reduce.5.cloned.1.call-done = f32[80,256]{1,0:T(8,128)} async-done(((f32[80,256]{1,0:T(8,128)}), f32[80,256]{1,0:T(8,128)}) %all-reduce.5.cloned.1.call-update) | async-done | bytes 81936 | tf_op jit(solution)/shard_map/psum | solution.py:54
  317.0 0.9 reduce_sum.72
  317.9 0.9 multiply_reduce_fusion.7
  318.9 19.8 %convolution_multiply_fusion.3 = f32[256,16384]{1,0:T(8,128)} fusion(f32[80,16384]{1,0:T(8,128)} %all_to_all.31, f32[256]{0:T(256)S(1)} %bitcast.102, f32[16384]{0:T(1024)S(1)} %add_convert_fusion, f32[80,256]{1,0:T(8,128)} %all-reduce.5.cloned.1.call-done, f32[256]{0:T(256)S(1)} %get-tuple-element.33, f32[256]{0:T(256)S(1)} %broadcast_multiply_fusion.7), kind=kOutput, calls=%fused_computation.7 | convolution fusion | flops 4051738624 | bytes 22170624 | tf_op jit(solution)/shard_map/dot_general | solution.py:35
  338.8 15.2 %convolution_add_fusion.3 = f32[80,16384]{1,0:T(8,128)} fusion(f32[80,16384]{1,0:T(8,128)S(1)} %bitcast.70, f32[256,16384]{1,0:T(8,128)} %convolution_multiply_fusion.3, f32[80,256]{1,0:T(8,128)S(1)} %copy-done.1, f32[256]{0:T(256)S(1)} %bitcast.90, f32[256]{0:T(256)S(1)} %bitcast.89, f32[256]{0:T(256)S(1)} %broadcast_multiply_fusion.7), kind=kOutput, calls=%fused_computation.11 | convolution fusion | flops 4027904000 | bytes 27347968 | tf_op jit(solution)/shard_map/dot_general | solution.py:37
  353.9 7.9 copy.36
  361.9 58.2 %gather_fusion.1 = f32[16384,80]{1,0:T(8,128)} fusion(f32[80,16384]{0,1:T(8,128)} %copy.36, s32[16384]{0:T(1024)S(1)} %fusion.25), kind=kCustom, calls=%fused_computation.1.clone | custom fusion | bytes 10551296 | tf_op jit(solution)/shard_map/jit(_take)/gather | solution.py:50
  420.0 6.9 multiply_reduce_fusion.2
  426.9 0.7 copy.51
  427.6 0.5 all-reduce.9.cloned.1.call-start
  428.3 134.8 %all-reduce.7.cloned.1.call-done = f32[80,256]{1,0:T(8,128)} async-done(((f32[80,256]{1,0:T(8,128)}), f32[80,256]{1,0:T(8,128)}) %all-reduce.7.cloned.1.call-update) | async-done | bytes 81936 | tf_op jit(solution)/shard_map/psum | solution.py:54
  563.0 0.9 reduce_sum.74
  564.0 0.9 multiply_reduce_fusion.6
  564.9 19.8 %convolution_multiply_fusion.2 = f32[256,16384]{1,0:T(8,128)} fusion(f32[80,16384]{1,0:T(8,128)} %convolution_add_fusion.3, f32[256]{0:T(256)S(1)} %bitcast.101, f32[16384]{0:T(1024)S(1)} %add_convert_fusion, f32[80,256]{1,0:T(8,128)} %all-reduce.7.cloned.1.call-done, f32[256]{0:T(256)S(1)} %get-tuple-element.31, f32[256]{0:T(256)S(1)} %broadcast_multiply_fusion.6), kind=kOutput, calls=%fused_computation.6 | convolution fusion | flops 4051738624 | bytes 22170624 | tf_op jit(solution)/shard_map/dot_general | solution.py:35
  584.8 15.2 %convolution_add_fusion.2 = f32[80,16384]{1,0:T(8,128)} fusion(f32[80,16384]{1,0:T(8,128)S(1)} %bitcast.74, f32[256,16384]{1,0:T(8,128)} %convolution_multiply_fusion.2, f32[80,256]{1,0:T(8,128)S(1)} %copy-done.3, f32[256]{0:T(256)S(1)} %bitcast.92, f32[256]{0:T(256)S(1)} %bitcast.91, f32[256]{0:T(256)S(1)} %broadcast_multiply_fusion.6), kind=kOutput, calls=%fused_computation.10 | convolution fusion | flops 4027904000 | bytes 27347968 | tf_op jit(solution)/shard_map/dot_general | solution.py:37
  599.9 7.9 copy.38
  607.9 58.2 %gather_fusion.2 = f32[16384,80]{1,0:T(8,128)} fusion(f32[80,16384]{0,1:T(8,128)} %copy.38, s32[16384]{0:T(1024)S(1)} %fusion.26), kind=kCustom, calls=%fused_computation.2.clone | custom fusion | bytes 10551296 | tf_op jit(solution)/shard_map/jit(_take)/gather | solution.py:50
  666.1 6.9 multiply_reduce_fusion.1
  672.9 0.7 copy.56
  674.0 135.0 %all-reduce.9.cloned.1.call-done = f32[80,256]{1,0:T(8,128)} async-done(((f32[80,256]{1,0:T(8,128)}), f32[80,256]{1,0:T(8,128)}) %all-reduce.9.cloned.1.call-update) | async-done | bytes 81936 | tf_op jit(solution)/shard_map/psum | solution.py:54
  809.0 0.9 reduce_sum.76
  809.9 0.9 multiply_reduce_fusion.5
  810.9 19.8 %convolution_multiply_fusion.1 = f32[256,16384]{1,0:T(8,128)} fusion(f32[80,16384]{1,0:T(8,128)} %convolution_add_fusion.2, f32[256]{0:T(256)S(1)} %bitcast.100, f32[16384]{0:T(1024)S(1)} %add_convert_fusion, f32[80,256]{1,0:T(8,128)} %all-reduce.9.cloned.1.call-done, f32[256]{0:T(256)S(1)} %get-tuple-element.29, f32[256]{0:T(256)S(1)} %broadcast_multiply_fusion.5), kind=kOutput, calls=%fused_computation.5 | convolution fusion | flops 4051738624 | bytes 22170624 | tf_op jit(solution)/shard_map/dot_general | solution.py:35
  830.7 15.2 %convolution_add_fusion.1 = f32[80,16384]{1,0:T(8,128)} fusion(f32[80,16384]{1,0:T(8,128)S(1)} %bitcast.72, f32[256,16384]{1,0:T(8,128)} %convolution_multiply_fusion.1, f32[80,256]{1,0:T(8,128)S(1)} %copy-done.2, f32[256]{0:T(256)S(1)} %bitcast.94, f32[256]{0:T(256)S(1)} %bitcast.93, f32[256]{0:T(256)S(1)} %broadcast_multiply_fusion.5), kind=kOutput, calls=%fused_computation.9 | convolution fusion | flops 4027904000 | bytes 27347968 | tf_op jit(solution)/shard_map/dot_general | solution.py:37
  845.9 7.9 copy.40
  853.9 58.2 %gather_fusion.3 = f32[16384,80]{1,0:T(8,128)} fusion(f32[80,16384]{0,1:T(8,128)} %copy.40, s32[16384]{0:T(1024)S(1)} %fusion.27), kind=kCustom, calls=%fused_computation.3.clone | custom fusion | bytes 10551296 | tf_op jit(solution)/shard_map/jit(_take)/gather | solution.py:50
  912.0 6.9 multiply_reduce_fusion
  918.9 0.7 copy.61
  919.6 135.4 %all-reduce.11.cloned.1.call-done = f32[80,256]{1,0:T(8,128)} async-done(((f32[80,256]{1,0:T(8,128)}), f32[80,256]{1,0:T(8,128)}) %all-reduce.11.cloned.1.call-update) | async-done | bytes 81936 | tf_op jit(solution)/shard_map/psum | solution.py:54
  1055.0 0.9 reduce_sum.78
  1055.9 0.9 multiply_reduce_fusion.4
  1056.9 20.0 %convolution_multiply_fusion = f32[256,16384]{1,0:T(8,128)} fusion(f32[80,16384]{1,0:T(8,128)} %convolution_add_fusion.1, f32[256]{0:T(256)S(1)} %bitcast.99, f32[16384]{0:T(1024)S(1)} %add_convert_fusion, f32[80,256]{1,0:T(8,128)} %all-reduce.11.cloned.1.call-done, f32[256]{0:T(256)S(1)} %get-tuple-element.27, f32[256]{0:T(256)S(1)} %broadcast_multiply_fusion.4), kind=kOutput, calls=%fused_computation.4 | convolution fusion | flops 4051738624 | bytes 22170624 | tf_op jit(solution)/shard_map/dot_general | solution.py:35
  1077.0 15.2 %convolution_add_fusion = f32[80,16384]{1,0:T(8,128)} fusion(f32[80,16384]{1,0:T(8,128)S(1)} %bitcast.76, f32[256,16384]{1,0:T(8,128)} %convolution_multiply_fusion, f32[80,256]{1,0:T(8,128)S(1)} %copy-done.4, f32[256]{0:T(256)S(1)} %bitcast.88, f32[256]{0:T(256)S(1)} %bitcast.87, f32[256]{0:T(256)S(1)} %broadcast_multiply_fusion.4), kind=kOutput, calls=%fused_computation.8 | convolution fusion | flops 4027904000 | bytes 27347968 | tf_op jit(solution)/shard_map/dot_general | solution.py:37
  1092.1 4.7 all_to_all.32
  1096.9 75.2 %all_to_all.38 = f32[4,20,16384]{2,1,0:T(8,128)S(1)} all-to-all(f32[4,20,16384]{2,1,0:T(8,128)} %all_to_all.32), channel_id=1, replica_groups=mesh['var'=32,'mem'=4] {'mem'}, dimensions={0} | all-to-all | bytes 10485760 | tf_op jit(solution)/shard_map/all_to_all | solution.py:57
  1172.0 3.4 copy.41
  1175.4 1.5 pad.4
  1177.0 6.3 copy.66
  (80 shorter events, 1.9 us)
Async XLA Ops:
  21.9 5.5 copy-start
  21.9 5.7 copy-start.5
  21.9 76.5 %all-to-all-start = ((f32[20,4,16384]{2,0,1:T(8,128)}), f32[20,4,16384]{2,0,1:T(8,128)}, u32[]{:S(2)}, u32[]{:S(2)}) async-start(f32[20,4,16384]{2,0,1:T(8,128)} %copy.32), calls=%async_computation | async-start | bytes 12582912 | tf_op jit(solution)/shard_map/all_to_all | solution.py:45
  27.3 289.8 %all-reduce.5.cloned.1.call-start = ((), (), s32[]{:S(2)}) async-start(), calls=%async_computation.2 | async-start | bytes 163840 | tf_op jit(solution)/shard_map/psum | solution.py:54
  169.1 7.9 copy-start.6
  169.1 149.7 %copy-start.7 = (f32[4,256]{1,0:T(4,128)S(1)}, f32[4,256]{1,0:T(4,128)}, u32[]{:S(2)}) copy-start(f32[4,256]{1,0:T(4,128)} %param.12) | copy-start | bytes 12292
  169.1 149.7 %copy-start.8 = (f32[4,256]{1,0:T(4,128)S(1)}, f32[4,256]{1,0:T(4,128)}, u32[]{:S(2)}) copy-start(f32[4,256]{1,0:T(4,128)} %param.13) | copy-start | bytes 12292
  169.1 169.6 %slice-start = ((s8[5242880]{0:T(1024)(128)(4,1)}), s8[1048576]{0:T(1024)(128)(4,1)S(1)}, s32[]{:S(2)}) async-start(s8[5242880]{0:T(1024)(128)(4,1)} %bitcast.69), calls=%async_computation.6 | async-start | bytes 2097152
  176.8 386.3 %all-reduce.7.cloned.1.call-start = ((), (), s32[]{:S(2)}) async-start(), calls=%async_computation.3 | async-start | bytes 163840 | tf_op jit(solution)/shard_map/psum | solution.py:54
  318.9 19.8 %slice-start.1 = ((s8[5242880]{0:T(1024)(128)(4,1)}), s8[4194304]{0:T(1024)(128)(4,1)S(1)}, s32[]{:S(2)}) async-start(s8[5242880]{0:T(1024)(128)(4,1)} %bitcast.69), calls=%async_computation.7 | async-start | bytes 8388608
  318.9 19.8 %copy-start.1 = (f32[80,256]{1,0:T(8,128)S(1)}, f32[80,256]{1,0:T(8,128)}, u32[]{:S(2)}) copy-start(f32[80,256]{1,0:T(8,128)} %all-reduce.5.cloned.1.call-done) | copy-start | bytes 245764
  420.0 164.7 %slice-start.4 = ((s8[5242880]{0:T(1024)(128)(4,1)}), s8[1048576]{0:T(1024)(128)(4,1)S(1)}, s32[]{:S(2)}) async-start(s8[5242880]{0:T(1024)(128)(4,1)} %bitcast.73), calls=%async_computation.10 | async-start | bytes 2097152
  427.6 381.4 %all-reduce.9.cloned.1.call-start = ((), (), s32[]{:S(2)}) async-start(), calls=%async_computation.4 | async-start | bytes 163840 | tf_op jit(solution)/shard_map/psum | solution.py:54
  564.9 19.8 %slice-start.5 = ((s8[5242880]{0:T(1024)(128)(4,1)}), s8[4194304]{0:T(1024)(128)(4,1)S(1)}, s32[]{:S(2)}) async-start(s8[5242880]{0:T(1024)(128)(4,1)} %bitcast.73), calls=%async_computation.11 | async-start | bytes 8388608
  564.9 19.8 %copy-start.3 = (f32[80,256]{1,0:T(8,128)S(1)}, f32[80,256]{1,0:T(8,128)}, u32[]{:S(2)}) copy-start(f32[80,256]{1,0:T(8,128)} %all-reduce.7.cloned.1.call-done) | copy-start | bytes 245764
  666.0 164.7 %slice-start.2 = ((s8[5242880]{0:T(1024)(128)(4,1)}), s8[1048576]{0:T(1024)(128)(4,1)S(1)}, s32[]{:S(2)}) async-start(s8[5242880]{0:T(1024)(128)(4,1)} %bitcast.71), calls=%async_computation.8 | async-start | bytes 2097152
  673.6 381.4 %all-reduce.11.cloned.1.call-start = ((), (), s32[]{:S(2)}) async-start(), calls=%async_computation.5 | async-start | bytes 163840 | tf_op jit(solution)/shard_map/psum | solution.py:54
  810.9 19.8 %slice-start.3 = ((s8[5242880]{0:T(1024)(128)(4,1)}), s8[4194304]{0:T(1024)(128)(4,1)S(1)}, s32[]{:S(2)}) async-start(s8[5242880]{0:T(1024)(128)(4,1)} %bitcast.71), calls=%async_computation.9 | async-start | bytes 8388608
  810.9 19.8 %copy-start.2 = (f32[80,256]{1,0:T(8,128)S(1)}, f32[80,256]{1,0:T(8,128)}, u32[]{:S(2)}) copy-start(f32[80,256]{1,0:T(8,128)} %all-reduce.9.cloned.1.call-done) | copy-start | bytes 245764
  912.0 164.9 %slice-start.6 = ((s8[5242880]{0:T(1024)(128)(4,1)}), s8[1048576]{0:T(1024)(128)(4,1)S(1)}, s32[]{:S(2)}) async-start(s8[5242880]{0:T(1024)(128)(4,1)} %bitcast.75), calls=%async_computation.12 | async-start | bytes 2097152
  1056.9 20.1 %slice-start.7 = ((s8[5242880]{0:T(1024)(128)(4,1)}), s8[4194304]{0:T(1024)(128)(4,1)S(1)}, s32[]{:S(2)}) async-start(s8[5242880]{0:T(1024)(128)(4,1)} %bitcast.75), calls=%async_computation.13 | async-start | bytes 8388608
  1056.9 20.1 %copy-start.4 = (f32[80,256]{1,0:T(8,128)S(1)}, f32[80,256]{1,0:T(8,128)}, u32[]{:S(2)}) copy-start(f32[80,256]{1,0:T(8,128)} %all-reduce.11.cloned.1.call-done) | copy-start | bytes 245764
Sparse Core Ops, SparseCore 0:
  176.9 140.0 all-reduce.4
  427.8 135.2 all-reduce.6
  673.8 135.2 all-reduce.8
  919.7 135.2 all-reduce.10
where the time goes:
time: 1200 us; the launch traced here: 1190 us
  waiting for transfers between devices  615 us (51%)
  local copies, waits for them, and re-layouts  304 us (25%)
  matrix products  140 us (12%)
  blocking collectives  75.2 us (6%)
  other arithmetic  35.1 us (3%)
  between operations  13.8 us (1%)
    psum x4, waiting for transfers between devices, shards(): prior_ens = lax.psum(partial_ens, ('var', 'mem'))  545 us
    gather x4, local copies, waits for them, and re-layouts, shards(): picked = jnp.take(columns, clipped.reshape(-1), axis=1)  233 us
    dot_general x4, matrix products, increment_block(): slopes = jnp.dot(regress.T, cell_block, precision=HIGHEST_PREC)  79.5 us
    all_to_all x1, blocking collectives, shards(): lax.all_to_all(columns, 'mem', split_axis=0, concat_axis=1, tiled=True)  75.2 us
    all_to_all x1, waiting for transfers between devices, shards(): lax.all_to_all(ensemble, 'mem', split_axis=1, concat_axis=0, tiled=True)  69.9 us
    dot_general x4, matrix products, increment_block(): return cell_block + jnp.dot(increments, slopes, precision=HIGHEST_PREC)  60.7 us
    all_to_all x4, local copies, waits for them, and re-layouts, shards(): lax.all_to_all(ensemble, 'mem', split_axis=1, concat_axis=0, tiled=True)  27.9 us
    unnamed x8, other arithmetic  27.4 us
  transfers between devices with their start and end apart: 5, of which 5 were waited for; matrix products, arithmetic and copies ran while one was open for 0% of the time, Pallas kernels for 0%

commit v1 on v0

--- a/solution.py
+++ b/solution.py
@@ -1,15 +1,21 @@
+import functools
+
 import jax
 import jax.numpy as jnp
 from jax import lax
+from jax.experimental import pallas as pl
+from jax.experimental.pallas import tpu as pltpu
 from jax.sharding import PartitionSpec as P
 
 CELLS = 16384
 NBATCH = 4
 LRAD = 4
-
-
+EPSILON = 1e-06
+LANES = 128
 HIGHEST_PREC = lax.Precision.HIGHEST
-EPSILON = 1e-06
+MESH = pl.DeviceIdType.MESH
+BF16 = jnp.bfloat16
+F32 = jnp.float32
 
 
 def innovations(prior_ens, obs_now, error_var):
@@ -25,19 +31,19 @@
     return (increments, regress)
 
 
-def taper_weights(positions, centers):
-    centre_pos = (centers.astype(jnp.float32) + 0.5) * CELLS
-    distance = jnp.abs(positions[None, :] - centre_pos[:, None]) / (LRAD * CELLS)
+def taper_weights(positions, centers, cells):
+    centre_pos = (centers.astype(jnp.float32) + 0.5) * cells
+    distance = jnp.abs(positions[None, :] - centre_pos[:, None]) / (LRAD * cells)
     return jnp.maximum(0.0, 1.0 - distance)
 
 
-def increment_block(cell_block, positions, increments, regress, centers):
+def increment_block(cell_block, positions, increments, regress, centers, cells):
     slopes = jnp.dot(regress.T, cell_block, precision=HIGHEST_PREC)
-    slopes = slopes * taper_weights(positions, centers)
+    slopes = slopes * taper_weights(positions, centers, cells)
     return cell_block + jnp.dot(increments, slopes, precision=HIGHEST_PREC)
 
 
-def shards(ensemble, ray_cells, ray_weights, ray_centers, obs_values, obs_var):
+def plain(ensemble, ray_cells, ray_weights, ray_centers, obs_values, obs_var):
     groups = lax.axis_size("mem")
     cell_count = ensemble.shape[1] // groups
     anchor = (lax.axis_index("var") * groups + lax.axis_index("mem")) * cell_count
@@ -53,9 +59,452 @@
         partial_ens = jnp.einsum("mjk,jk->mj", picked, weights_here, precision=HIGHEST_PREC)
         prior_ens = lax.psum(partial_ens, ("var", "mem"))
         increments, regress = innovations(prior_ens, obs_values[batch_index], obs_var[batch_index])
-        columns = increment_block(columns, positions, increments, regress, ray_centers[batch_index])
-    ensemble = lax.all_to_all(columns, "mem", split_axis=0, concat_axis=1, tiled=True)
-    return ensemble
+        columns = increment_block(columns, positions, increments, regress, ray_centers[batch_index], cell_count)
+    return lax.all_to_all(columns, "mem", split_axis=0, concat_axis=1, tiled=True)
+
+
+def lanes_of(shape):
+    return lax.broadcasted_iota(jnp.int32, shape, 1)
+
+
+def squeeze_rows(packed, weight, mask):
+    rows = packed.shape[0]
+    lane = lanes_of(packed.shape)
+    marks = mask.astype(BF16)
+    upper = lax.broadcasted_iota(jnp.int32, (LANES, LANES), 0) < lanes_of((LANES, LANES))
+    before = jnp.dot(marks, upper.astype(BF16), preferred_element_type=F32)
+    count = jnp.dot(marks, jnp.ones((LANES, LANES), BF16), preferred_element_type=F32).astype(jnp.int32)
+    gap = jnp.where(mask, lane - before.astype(jnp.int32), -1)
+    for bit in range(7):
+        step = 1 << bit
+        moved_gap = pltpu.roll(gap, LANES - step, 1)
+        take = (moved_gap >= 0) & ((moved_gap & step) != 0)
+        keep = (gap >= 0) & ((gap & step) == 0)
+        packed = jnp.where(take, pltpu.roll(packed, LANES - step, 1), packed)
+        weight = jnp.where(take, pltpu.roll(weight, LANES - step, 1), weight)
+        gap = jnp.where(take, moved_gap, jnp.where(keep, gap, -1))
+    while rows > 8:
+        rows //= 2
+        first, second = count[:rows], count[rows:]
+        p2, w2 = packed[rows:], weight[rows:]
+        for bit in range(7):
+            step = 1 << bit
+            far = (first & step) != 0
+            p2 = jnp.where(far, pltpu.roll(p2, step, 1), p2)
+            w2 = jnp.where(far, pltpu.roll(w2, step, 1), w2)
+        own = lanes_of(first.shape) < first
+        packed = jnp.where(own, packed[:rows], p2)
+        weight = jnp.where(own, weight[:rows], w2)
+        count = first + second
+    return packed, weight, count
+
+
+def pick_kernel(n_mem, kcells, cells_ref, weights_ref, ens_ref, g_ref, ray_ref, place_ref,
+                ens_v, xt, graw, w_v, n_v, list_s, n_s, ens_sem, list_sem):
+    members, span = ens_ref.shape
+    batch_rows = cells_ref.shape[0] // NBATCH
+    load = pltpu.make_async_copy(ens_ref, ens_v, ens_sem)
+    load.start()
+    base = lax.axis_index("var") * span
+    for batch in range(NBATCH):
+        rows = pl.ds(batch * batch_rows, batch_rows)
+        place = cells_ref[rows, :] - base
+        mask = (place >= 0) & (place < span)
+        row = lax.broadcasted_iota(jnp.int32, place.shape, 0)
+        ray = row * (LANES // kcells) + lanes_of(place.shape) // kcells
+        packed, weight, count = squeeze_rows(jnp.bitwise_or(ray << 16, place & 0xFFFF), weights_ref[rows, :], mask)
+        valid = lanes_of(count.shape) < count
+        out_rows = pl.ds(batch * 8, 8)
+        place_ref[out_rows, :] = jnp.where(valid, packed & 0xFFFF, 0)
+        ray_ref[out_rows, :] = jnp.where(valid, packed >> 16, -1)
+        w_v[out_rows, :] = jnp.where(valid, weight, 0.0)
+        n_v[out_rows, :] = count
+    to_list = pltpu.make_async_copy(place_ref, list_s, list_sem.at[0])
+    to_count = pltpu.make_async_copy(n_v, n_s, list_sem.at[1])
+    to_list.start()
+    to_count.start()
+    load.wait()
+
+    def turn(group, carry):
+        tiles = []
+        for part in range(4):
+            at = pl.ds(pl.multiple_of(group * 4 * LANES + part * LANES, LANES), LANES)
+            tiles.append(ens_v[:, at])
+            tiles.append(jnp.zeros((32 - members, LANES), F32))
+        xt[pl.ds(pl.multiple_of(group * LANES, LANES), LANES), :] = jnp.concatenate(tiles, axis=0).T
+        return carry
+
+    lax.fori_loop(0, span // (4 * LANES), turn, 0)
+    to_list.wait()
+    to_count.wait()
+
+    def gather_row(row, carry):
+        def gather_eight(block, inner):
+            for unit in range(8):
+                slot = block * 8 + unit
+                place = list_s[row, slot]
+                source = ((place >> 9) << 7) | (place & 127)
+                graw[pl.ds(row * LANES + slot, 1), :] = xt[pl.ds(source, 1), :]
+            return inner
+
+        lax.fori_loop(0, (n_s[row, 0] + 7) // 8, gather_eight, 0)
+        return carry
+
+    lax.fori_loop(0, NBATCH * 8, gather_row, 0)
+
+    per_mem = 8 // n_mem
+    for row in range(NBATCH * 8):
+        batch, lane_group = row // 8, row % 8
+        owner, inner = lane_group // per_mem, lane_group % per_mem
+        raw = graw[pl.ds(row * LANES, LANES), :].T
+        part = (place_ref[pl.ds(row, 1), :] >> 7) & 3
+        total = jnp.zeros((24, LANES), F32)
+        for piece in range(4):
+            total = jnp.where(part == piece, raw[32 * piece:32 * piece + 24, :], total)
+        total = jnp.where(ray_ref[pl.ds(row, 1), :] >= 0, total, 0.0) * w_v[pl.ds(row, 1), :]
+        at = ((owner * NBATCH + batch) * per_mem + inner) * LANES
+        g_ref[:, pl.ds(at, LANES)] = total
+
+
+def pick(ensemble, ray_cells, ray_weights, n_mem):
+    members, span = ensemble.shape
+    kcells = ray_cells.shape[2]
+    rows = ray_cells.size // LANES
+    chunks = NBATCH * 8
+    vmem = pl.BlockSpec(memory_space=pltpu.VMEM)
+    return pl.pallas_call(
+        functools.partial(pick_kernel, n_mem, kcells),
+        out_shape=(
+            jax.ShapeDtypeStruct((24, chunks * LANES), F32),
+            jax.ShapeDtypeStruct((chunks, LANES), jnp.int32),
+            jax.ShapeDtypeStruct((chunks, LANES), jnp.int32),
+        ),
+        in_specs=[vmem, vmem, pl.BlockSpec(memory_space=pl.ANY)],
+        out_specs=(vmem, vmem, vmem),
+        scratch_shapes=[
+            pltpu.VMEM((members, span), F32),
+            pltpu.VMEM((span // 4, LANES), F32),
+            pltpu.VMEM((chunks * LANES, LANES), F32),
+            pltpu.VMEM((chunks, LANES), F32),
+            pltpu.VMEM((chunks, LANES), jnp.int32),
+            pltpu.SMEM((chunks, LANES), jnp.int32),
+            pltpu.SMEM((chunks, LANES), jnp.int32),
+            pltpu.SemaphoreType.DMA,
+            pltpu.SemaphoreType.DMA((2,)),
+        ],
+        compiler_params=pltpu.CompilerParams(vmem_limit_bytes=48 << 20),
+        name="pick",
+    )(ray_cells.reshape(rows, LANES), ray_weights.reshape(rows, LANES), ensemble)
+
+
+def high_dot(a, b):
+    return jnp.dot(a, b, precision=HIGHEST_PREC, preferred_element_type=F32)
+
+
+def main_kernel(dims, ens_ref, g_ref, ray_ref, place_ref, par_ref, out_ref,
+                xf, res, xr, rsb, xb, agb, part_v, inc_v, reg_v, dpoly, dhi, dlo,
+                mini_s, mini_r, fwd_s, fwd_r, own_sem, red_s, red_r, back_s, back_r):
+    n_var, n_mem, members, cells, nobs, n_chunk = dims
+    group = members // n_mem
+    wide = 24 * n_mem
+    slots = 8 // n_mem * LANES
+    all_slots = NBATCH * slots
+    width = cells // n_chunk
+    rays_here = nobs // n_var
+    p, q = lax.axis_index("var"), lax.axis_index("mem")
+
+    def var_peer(k):
+        return {"var": lax.rem(p + k, n_var)}
+
+    def mem_peer(k):
+        return {"mem": lax.rem(q + k, n_mem)}
+
+    barrier = pltpu.get_barrier_semaphore()
+
+    def greet(k, carry):
+        pl.semaphore_signal(barrier, inc=1, device_id=var_peer(k), device_id_type=MESH)
+        return carry
+
+    lax.fori_loop(1, n_var, greet, 0)
+    for k in range(1, n_mem):
+        pl.semaphore_signal(barrier, inc=1, device_id=mem_peer(k), device_id_type=MESH)
+    pl.semaphore_wait(barrier, n_var - 1 + n_mem - 1)
+
+    mini = []
+    for k in range(1, n_mem):
+        there = lax.rem(q + k, n_mem)
+        copy = pltpu.make_async_remote_copy(
+            src_ref=g_ref.at[:, pl.ds(pl.multiple_of(there * all_slots, LANES), all_slots)],
+            dst_ref=xr.at[q],
+            send_sem=mini_s.at[k], recv_sem=mini_r.at[k],
+            device_id=mem_peer(k), device_id_type=MESH)
+        copy.start()
+        mini.append(copy)
+    own = pltpu.make_async_copy(ens_ref.at[:, pl.ds(pl.multiple_of(q * cells, LANES), cells)], xf.at[q], own_sem.at[0])
+    own.start()
+
+    def forward(k, chunk):
+        there = lax.rem(q + k, n_mem)
+        return pltpu.make_async_remote_copy(
+            src_ref=ens_ref.at[:, pl.ds(pl.multiple_of(there * cells + chunk * width, LANES), width)],
+            dst_ref=xf.at[q, :, pl.ds(pl.multiple_of(chunk * width, LANES), width)],
+            send_sem=fwd_s.at[k, chunk], recv_sem=fwd_r.at[k, chunk],
+            device_id=mem_peer(k), device_id_type=MESH)
+
+    def start_forward(chunk, carry):
+        for k in (2, 1, 3):
+            forward(k, chunk).start()
+        return carry
+
+    lax.fori_loop(0, n_chunk, start_forward, 0)
+
+    xr[q] = g_ref[:, pl.ds(pl.multiple_of(q * all_slots, LANES), all_slots)]
+    lane = lanes_of((1, LANES))
+    real_lane = (lax.rem(lane, 24) < group) & (lane < wide)
+    block = p * n_mem + q
+    per_mem = 8 // n_mem
+
+    def meta_row(ref, batch):
+        rows = [ref[pl.ds(batch * 8 + q * per_mem + inner, 1), :] for inner in range(per_mem)]
+        return jnp.concatenate(rows, axis=1)
+
+    ray_rows = [meta_row(ray_ref, b) for b in range(NBATCH)]
+    pos_rows = [(meta_row(place_ref, b) + p * (n_mem * cells)).astype(F32) for b in range(NBATCH)]
+    ray_column = lax.broadcasted_iota(jnp.int32, (nobs, 1), 0)
+    part_v[...] = jnp.zeros_like(part_v)
+    for copy in mini:
+        copy.wait()
+
+    def own_rows():
+        return pl.ds(pl.multiple_of(p * rays_here, rays_here), rays_here)
+
+    def start_reduce(batch):
+        state = xr[:, :, pl.ds(batch * slots, slots)].reshape(wide, slots)
+        chosen = (ray_rows[batch] == ray_column).astype(F32)
+        part_v[batch, :, pl.ds(0, wide)] = high_dot(chosen, state.T)
+
+        def send(k, carry):
+            there = lax.rem(p + k, n_var)
+            pltpu.make_async_remote_copy(
+                src_ref=part_v.at[batch, pl.ds(pl.multiple_of(there * rays_here, rays_here), rays_here)],
+                dst_ref=rsb.at[batch, p],
+                send_sem=red_s.at[batch, 0], recv_sem=red_r.at[batch, 0],
+                device_id=var_peer(k), device_id_type=MESH).start()
+            return carry
+
+        lax.fori_loop(1, n_var, send, 0)
+        rsb[batch, p] = part_v[batch, own_rows(), :]
+
+    def finish_reduce(batch):
+        landed = rsb.at[batch, pl.ds(0, n_var - 1)]
+        pltpu.make_async_remote_copy(
+            src_ref=landed, dst_ref=landed, send_sem=red_s.at[batch, 0], recv_sem=red_r.at[batch, 0],
+            device_id=var_peer(1), device_id_type=MESH).wait()
+        xb[batch, q] = jnp.sum(rsb[batch], axis=0)
+        across = []
+        for k in range(1, n_mem):
+            copy = pltpu.make_async_remote_copy(
+                src_ref=xb.at[batch, q], dst_ref=xb.at[batch, q],
+                send_sem=red_s.at[batch, k], recv_sem=red_r.at[batch, k],
+                device_id=mem_peer(k), device_id_type=MESH)
+            copy.start()
+            across.append(copy)
+        for copy in across:
+            copy.wait()
+        agb[batch, own_rows(), :] = jnp.sum(xb[batch], axis=0)
+        mine = agb.at[batch, own_rows()]
+
+        def send(k, carry):
+            pltpu.make_async_remote_copy(
+                src_ref=mine, dst_ref=mine,
+                send_sem=red_s.at[batch, n_mem], recv_sem=red_r.at[batch, n_mem],
+                device_id=var_peer(k), device_id_type=MESH).start()
+            return carry
+
+        lax.fori_loop(1, n_var, send, 0)
+        landed = agb.at[batch, pl.ds(0, nobs - rays_here)]
+        pltpu.make_async_remote_copy(
+            src_ref=landed, dst_ref=landed, send_sem=red_s.at[batch, n_mem], recv_sem=red_r.at[batch, n_mem],
+            device_id=var_peer(1), device_id_type=MESH).wait()
+
+    def innovate(batch):
+        prior = agb[batch]
+        obs = par_ref[:, NBATCH + batch:NBATCH + batch + 1]
+        error_var = par_ref[:, 2 * NBATCH + batch:2 * NBATCH + batch + 1]
+        mean = jnp.sum(prior, axis=1, keepdims=True) / members
+        anomaly = jnp.where(real_lane, prior - mean, 0.0)
+        variance = jnp.sum(anomaly * anomaly, axis=1, keepdims=True) / (members - 1) + EPSILON
+        total_var = variance + error_var
+        post_mean = (mean * error_var + obs * variance) / total_var
+        shrink = jnp.sqrt(error_var / total_var)
+        increments = jnp.where(real_lane, post_mean - mean + (shrink - 1.0) * anomaly, 0.0)
+        inc_v[...] = increments.T
+        reg_v[...] = anomaly / ((members - 1) * variance)
+
+    def centre_pos(batch):
+        return (par_ref[:, batch:batch + 1] + 0.5) * cells
+
+    def taper_at(batch, positions):
+        return 1.0 - jnp.abs(positions - centre_pos(batch)) / (LRAD * cells)
+
+    def update_mini(batch):
+        for later in range(batch + 1, NBATCH):
+            at = pl.ds(later * slots, slots)
+            state = xr[:, :, at].reshape(wide, slots)
+            slopes = high_dot(reg_v[:, 0:wide], state)
+            slopes = slopes * jnp.maximum(taper_at(batch, pos_rows[later]), 0.0)
+            state = state + high_dot(inc_v[0:wide, :], slopes)
+            xr[:, :, at] = state.reshape(n_mem, 24, slots)
+
+    def compose(batch):
+        for half in range(2):
+            start = (block * cells + half * (cells // 2)).astype(F32)
+            near, far = taper_at(batch, start), taper_at(batch, start + cells // 2)
+            inside = near + far > 0.0
+            alpha = jnp.where(inside, near, 0.0)
+            beta = jnp.where(inside, far - near, 0.0)
+            regress = reg_v[...]
+            both = jnp.concatenate([regress * alpha, regress * beta], axis=1)
+            ab = high_dot(inc_v[0:wide, :], both)
+            a, b = ab[:, :LANES], ab[:, LANES:]
+            if batch == 0:
+                dpoly[half, 0], dpoly[half, 1] = a, b
+                continue
+            old = jnp.concatenate([dpoly[half, k] for k in range(batch + 1)], axis=1)
+            left = jnp.concatenate([a[:, 0:wide], b[:, 0:wide]], axis=0)
+            made = high_dot(left, old)
+            for k in range(batch + 2):
+                total = a if k == 0 else b if k == 1 else jnp.zeros_like(a)
+                if k <= batch:
+                    total = total + dpoly[half, k] + made[:wide, k * LANES:(k + 1) * LANES]
+                if k >= 1:
+                    total = total + made[wide:, (k - 1) * LANES:k * LANES]
+                dpoly[half, k] = total
+
+    start_reduce(0)
+    for batch in range(NBATCH):
+        finish_reduce(batch)
+        innovate(batch)
+        update_mini(batch)
+        if batch + 1 < NBATCH:
+            start_reduce(batch + 1)
+        compose(batch)
+
+    terms = NBATCH + 1
+    for half in range(2):
+        for k in range(terms):
+            value = dpoly[half, k][:, 0:wide]
+            high = value.astype(BF16)
+            dhi[half, pl.ds(k * wide, wide), :] = high
+            dlo[half, pl.ds(k * wide, wide), :] = (value - high.astype(F32)).astype(BF16)
+
+    own.wait()
+
+    def back(k, chunk):
+        there = lax.rem(q + k, n_mem)
+        return pltpu.make_async_remote_copy(
+            src_ref=res.at[there, :, pl.ds(pl.multiple_of(chunk * width, LANES), width)],
+            dst_ref=out_ref.at[:, pl.ds(pl.multiple_of(q * cells + chunk * width, LANES), width)],
+            send_sem=back_s.at[k], recv_sem=back_r.at[k],
+            device_id=mem_peer(k), device_id_type=MESH)
+
+    pad = jnp.zeros((24 - group, width), F32)
+
+    def apply(chunk, carry):
+        for k in (2, 1, 3):
+            forward(k, chunk).wait()
+        half = chunk // (n_chunk // 2)
+        at = pl.ds(pl.multiple_of(chunk * width, LANES), width)
+        pieces = []
+        for i in range(n_mem):
+            pieces += [xf[i, :, at], pad]
+        x = jnp.concatenate(pieces, axis=0)
+        high = x.astype(BF16)
+        low = (x - high.astype(F32)).astype(BF16)
+        big, small = dhi[half], dlo[half]
+        y = jnp.dot(big, high, preferred_element_type=F32)
+        y = y + jnp.dot(big, low, preferred_element_type=F32)
+        y = y + jnp.dot(small, high, preferred_element_type=F32)
+        t = (lanes_of((1, width)) + (chunk - half * (n_chunk // 2)) * width).astype(F32) * (2.0 / cells)
+        total = y[(terms - 1) * wide:]
+        for k in range(terms - 2, -1, -1):
+            total = y[k * wide:(k + 1) * wide] + t * total
+        total = x + total
+        for i in range(n_mem):
+            res[i, :, at] = total[24 * i:24 * i + group]
+        for k in (2, 1, 3):
+            back(k, chunk).start()
+        return carry
+
+    lax.fori_loop(0, n_chunk, apply, 0)
+    mine = pl.ds(pl.multiple_of(q * cells, LANES), cells)
+    keep = pltpu.make_async_copy(res.at[q], out_ref.at[:, mine], own_sem.at[1])
+    keep.start()
+    for k in range(1, n_mem):
+        source = lax.rem(q + n_mem - k, n_mem)
+        landed = out_ref.at[:, pl.ds(pl.multiple_of(source * cells, LANES), cells)]
+        pltpu.make_async_remote_copy(
+            src_ref=res.at[lax.rem(q + k, n_mem)], dst_ref=landed, send_sem=back_s.at[k], recv_sem=back_r.at[k],
+            device_id=mem_peer(k), device_id_type=MESH).wait()
+    keep.wait()
+
+
+def assimilate(ensemble, picked, rays, places, params, n_var, n_mem):
+    group, span = ensemble.shape
+    cells = span // n_mem
+    nobs = params.shape[0]
+    n_chunk = min(16, cells // 256)
+    wide = 24 * n_mem
+    all_slots = NBATCH * 8 // n_mem * LANES
+    vmem = pl.BlockSpec(memory_space=pltpu.VMEM)
+    anywhere = pl.BlockSpec(memory_space=pl.ANY)
+    dma = pltpu.SemaphoreType.DMA
+    dims = (n_var, n_mem, group * n_mem, cells, nobs, n_chunk)
+    return pl.pallas_call(
+        functools.partial(main_kernel, dims),
+        out_shape=jax.ShapeDtypeStruct((group, span), F32),
+        in_specs=[anywhere, vmem, vmem, vmem, vmem],
+        out_specs=anywhere,
+        scratch_shapes=[
+            pltpu.VMEM((n_mem, group, cells), F32),
+            pltpu.VMEM((n_mem, group, cells), F32),
+            pltpu.VMEM((n_mem, 24, all_slots), F32),
+            pltpu.VMEM((NBATCH, n_var, nobs // n_var, LANES), F32),
+            pltpu.VMEM((NBATCH, n_mem, nobs // n_var, LANES), F32),
+            pltpu.VMEM((NBATCH, nobs, LANES), F32),
+            pltpu.VMEM((NBATCH, nobs, LANES), F32),
+            pltpu.VMEM((LANES, nobs), F32),
+            pltpu.VMEM((nobs, LANES), F32),
+            pltpu.VMEM((2, NBATCH + 1, wide, LANES), F32),
+            pltpu.VMEM((2, (NBATCH + 1) * wide, wide), BF16),
+            pltpu.VMEM((2, (NBATCH + 1) * wide, wide), BF16),
+            dma((n_mem,)), dma((n_mem,)),
+            dma((n_mem, n_chunk)), dma((n_mem, n_chunk)),
+            dma((2,)),
+            dma((NBATCH, n_mem + 1)), dma((NBATCH, n_mem + 1)),
+            dma((n_mem,)), dma((n_mem,)),
+        ],
+        compiler_params=pltpu.CompilerParams(collective_id=1, has_side_effects=True, vmem_limit_bytes=48 << 20),
+        name="assimilate",
+    )(ensemble, picked, rays, places, params)
+
+
+def fast(ensemble, ray_cells, ray_weights, ray_centers, obs_values, obs_var):
+    n_var, n_mem = lax.axis_size("var"), lax.axis_size("mem")
+    picked, rays, places = pick(ensemble, ray_cells, ray_weights, n_mem)
+    params = jnp.concatenate([ray_centers.astype(F32), obs_values, obs_var], axis=0).T
+    return assimilate(ensemble, picked, rays, places, params, n_var, n_mem)
+
+
+def fits(ray_cells, span, n_var):
+    owner = ray_cells.reshape(NBATCH, -1, 8, LANES) // span
+    hits = owner[..., None] == jnp.arange(n_var, dtype=jnp.int32)
+    return jnp.max(jnp.sum(hits.astype(jnp.int32), axis=(1, 3))) <= LANES
+
+
+def shards(*arrays):
+    room = fits(arrays[1], arrays[0].shape[1], lax.axis_size("var"))
+    return lax.cond(room, fast, plain, *arrays)
 
 
 def solution(mesh):

time: 1200 us -> 267 us (0.22)
  waiting for transfers between devices: 615 us -> 0 us
  local copies, waits for them, and re-layouts: 304 us -> 9.86 us
  Pallas kernels: 0 us -> 239 us
  matrix products: 140 us -> 0 us
  blocking collectives: 75.2 us -> 0 us
  other arithmetic: 35.1 us -> 3.35 us
    psum x4 -> x0, waiting for transfers between devices: 545 us -> none  [shards(): prior_ens = lax.psum(partial_ens, ('var', 'mem'))]
    pallas_call x0 -> x2, Pallas kernels: none -> 239 us  [the longest x1 210 us: assimilate(): pl.pallas_call(functools.partial(main_kernel, dims), out_shape=jax.ShapeD...]
    gather x4 -> x0, local copies, waits for them, and re-layouts: 233 us -> none  [shards(): picked = jnp.take(columns, clipped.reshape(-1), axis=1)]
    dot_general x8 -> x0, matrix products: 140 us -> none  [the longest x4 79.5 us: increment_block(): slopes = jnp.dot(regress.T, cell_block, precision=HIGHEST_PREC)]
    all_to_all x1 -> x0, blocking collectives: 75.2 us -> none  [shards(): lax.all_to_all(columns, 'mem', split_axis=0, concat_axis=1, tiled=True)]
    all_to_all x1 -> x0, waiting for transfers between devices: 69.9 us -> none  [shards(): lax.all_to_all(ensemble, 'mem', split_axis=1, concat_axis=0, tiled=True)]
    all_to_all x6 -> x0, local copies, waits for them, and re-layouts: 36 us -> none  [the longest x4 27.9 us: shards(): lax.all_to_all(ensemble, 'mem', split_axis=1, concat_axis=0, tiled=True)]
    unnamed x8 -> x0, other arithmetic: 27.4 us -> none
  transfers between devices with their start and end apart: 5 -> 0, of which waited for: 5 -> 0; matrix products, arithmetic and copies ran while one was open for 0% -> 0% of each run, Pallas kernels for 0% -> 0%
where the time goes in v1:
time: 267 us; the launch traced here: 266 us
  Pallas kernels  239 us (90%)
  between operations  14.1 us (5%)
  local copies, waits for them, and re-layouts  9.86 us (4%)
  other arithmetic  3.35 us (1%)
    pallas_call x1, Pallas kernels, assimilate(): pl.pallas_call(functools.partial(main_kernel, dims), out_shape=jax.ShapeD...  210 us
    pallas_call x1, Pallas kernels, pick(): pl.pallas_call(functools.partial(pick_kernel, n_mem, kcells), out_shape=(...  28.1 us
    unnamed x2, local copies, waits for them, and re-layouts  7.03 us

profile of v1, /device:TPU:1, one launch (start us, length us, event | category | flops | bytes accessed | tf_op | source)
XLA Modules:
  0.0 266.4 jit_solution(18431627935156942217)
XLA Ops:
  6.5 1.1 copy.68
  7.7 0.1 reshape.289
  7.8 0.1 add_select_fusion
  8.0 1.2 convert_reduce_fusion
  9.1 0.6 reduce_max.9
  10.4 243.2 %conditional.1 = (f32[20,65536]{1,0:T(8,128)}) conditional(s32[]{:T(128)} %convert_element_type.49, (f32[20,65536]{1,0:T(8,128)}, s32[4,256,64]{1,2,0:T(8,128)}, f32[4,256,64]{1,2,0:T(8,128)}, f32[4,256]{1,0:T(4,128)}, f32[4,256]{1,0:T(4,128)}, /*index=5*/s32[4,256]{1,0:T(4,128)}) %tuple.12, (s32[4,256,64]{1,2,0:T(8,128)}, ...), branch_computations={%region_2.16_spmd, %region_15.17_spmd} | conditional | flops 32388296704 | bytes 524165920 | solution.py:507
  10.7 0.7 convert_element_type.45
  11.4 0.7 pad_maximum_fusion
  12.1 0.1 copy.61
  12.2 1.1 copy.72
  13.4 0.1 reshape.287.weights_ref
  13.5 1.1 copy.71
  14.7 0.1 reshape.286.cells_ref
  14.8 0.0 copy-start
  14.8 28.1 %pick.1 = (f32[24,4096]{1,0:T(8,128)S(1)}, s32[32,128]{1,0:T(8,128)S(1)}, s32[32,128]{1,0:T(8,128)S(1)}) custom-call(s32[512,128]{1,0:T(8,128)S(1)} %reshape.286.cells_ref, f32[512,128]{1,0:T(8,128)S(1)} %reshape.287.weights_ref, f32[20,65536]{1,0:T(8,128)} %get-tuple-element.39.ens_ref), custom_call_target="tpu_custom_call" | custom-call | tf_op jit(solution)/shard_map/cond/branch_1_fun/pick/pallas_call | solution.py:175
  42.9 0.0 copy-done
  42.9 210.5 %assimilate.1 = f32[20,65536]{1,0:T(8,128)} custom-call(f32[20,65536]{1,0:T(8,128)S(1)} %copy-done, f32[24,4096]{1,0:T(8,128)S(1)} %get-tuple-element.42.g_ref, s32[32,128]{1,0:T(8,128)S(1)} %get-tuple-element.43.ray_ref, s32[32,128]{1,0:T(8,128)S(1)} %get-tuple-element.44.place_ref, f32[256,12]{1,0:T(8,128)S(1)} %bitcast.82), custom_call_target="tpu_custom_call" | custom-call | tf_op jit(solution)/shard_map/cond/branch_1_fun/assimilate/pallas_call | solution.py:463
  253.7 5.9 %copy.89 = f32[20,65536]{1,0:T(8,128)} copy(f32[20,65536]{1,0:T(8,128)} %get-tuple-element.48) | data formatting | bytes 10485760
Async XLA Ops:
  14.8 28.1 %copy-start = (f32[20,65536]{1,0:T(8,128)S(1)}, f32[20,65536]{1,0:T(8,128)}, u32[]{:S(2)}) copy-start(f32[20,65536]{1,0:T(8,128)} %get-tuple-element.39.ens_ref) | copy-start | bytes 15728644 | tf_op jit(solution)/shard_map/cond

commit v2 on v1

v2 whole, which is shorter than its diff:
```python
import functools

import jax
import jax.numpy as jnp
from jax import lax
from jax.experimental import pallas as pl
from jax.experimental.pallas import tpu as pltpu
from jax.sharding import PartitionSpec as P

CELLS = 16384
NBATCH = 4
LRAD = 4
EPSILON = 1e-06
LANES = 128
HIGHEST_PREC = lax.Precision.HIGHEST
MESH = pl.DeviceIdType.MESH
N_CHUNK = 16
PACE = (2, 1, 2)
BF16 = jnp.bfloat16
F32 = jnp.float32


def innovations(prior_ens, obs_now, error_var):
    members = prior_ens.shape[0]
    prior_mean = jnp.mean(prior_ens, axis=0)
    anomaly = prior_ens - prior_mean
    variance = jnp.sum(anomaly * anomaly, axis=0) / (members - 1) + EPSILON
    total_var = variance + error_var
    post_mean = (prior_mean * error_var + obs_now * variance) / total_var
    shrink = jnp.sqrt(error_var / total_var)
    increments = post_mean - prior_mean + (shrink - 1.0) * anomaly
    regress = anomaly / ((members - 1) * variance)
    return (increments, regress)


def taper_weights(positions, centers, cells):
    centre_pos = (centers.astype(jnp.float32) + 0.5) * cells
    distance = jnp.abs(positions[None, :] - centre_pos[:, None]) / (LRAD * cells)
    return jnp.maximum(0.0, 1.0 - distance)


def increment_block(cell_block, positions, increments, regress, centers, cells):
    slopes = jnp.dot(regress.T, cell_block, precision=HIGHEST_PREC)
    slopes = slopes * taper_weights(positions, centers, cells)
    return cell_block + jnp.dot(increments, slopes, precision=HIGHEST_PREC)


def sum_everywhere(partial_ens):
    axes = ("var", "mem")
    count = lax.axis_size("var") * lax.axis_size("mem")
    members, rays = partial_ens.shape
    pieces = partial_ens.reshape(members, count, rays // count).transpose(1, 0, 2)
    total = jnp.sum(lax.all_to_all(pieces, axes, split_axis=0, concat_axis=0, tiled=True), axis=0)
    copies = jnp.broadcast_to(total, pieces.shape)
    whole = lax.all_to_all(copies, axes, split_axis=0, concat_axis=0, tiled=True)
    return whole.transpose(1, 0, 2).reshape(members, rays)


def plain(ensemble, ray_cells, ray_weights, ray_centers, obs_values, obs_var):
    groups = lax.axis_size("mem")
    cell_count = ensemble.shape[1] // groups
    anchor = (lax.axis_index("var") * groups + lax.axis_index("mem")) * cell_count
    positions = (anchor + jnp.arange(cell_count, dtype=jnp.int32)).astype(jnp.float32)
    columns = lax.all_to_all(ensemble, "mem", split_axis=1, concat_axis=0, tiled=True)
    for batch_index in range(NBATCH):
        offsets = ray_cells[batch_index] - anchor
        inside = (offsets >= 0) & (offsets < cell_count)
        clipped = jnp.clip(offsets, 0, cell_count - 1)
        picked = jnp.take(columns, clipped.reshape(-1), axis=1)
        picked = picked.reshape(columns.shape[0], clipped.shape[0], clipped.shape[1])
        weights_here = jnp.where(inside, ray_weights[batch_index], 0.0)
        partial_ens = jnp.einsum("mjk,jk->mj", picked, weights_here, precision=HIGHEST_PREC)
        prior_ens = sum_everywhere(partial_ens)
        increments, regress = innovations(prior_ens, obs_values[batch_index], obs_var[batch_index])
        columns = increment_block(columns, positions, increments, regress, ray_centers[batch_index], cell_count)
    return lax.all_to_all(columns, "mem", split_axis=0, concat_axis=1, tiled=True)


def lanes_of(shape):
    return lax.broadcasted_iota(jnp.int32, shape, 1)


def squeeze_rows(packed, weight, mask):
    rows = packed.shape[0]
    lane = lanes_of(packed.shape)
    marks = mask.astype(BF16)
    upper = lax.broadcasted_iota(jnp.int32, (LANES, LANES), 0) < lanes_of((LANES, LANES))
    before = jnp.dot(marks, upper.astype(BF16), preferred_element_type=F32)
    count = jnp.dot(marks, jnp.ones((LANES, LANES), BF16), preferred_element_type=F32).astype(jnp.int32)
    gap = jnp.where(mask, lane - before.astype(jnp.int32), -1)
    for bit in range(7):
        step = 1 << bit
        moved_gap = pltpu.roll(gap, LANES - step, 1)
        take = (moved_gap >= 0) & ((moved_gap & step) != 0)
        keep = (gap >= 0) & ((gap & step) == 0)
        packed = jnp.where(take, pltpu.roll(packed, LANES - step, 1), packed)
        weight = jnp.where(take, pltpu.roll(weight, LANES - step, 1), weight)
        gap = jnp.where(take, moved_gap, jnp.where(keep, gap, -1))
    while rows > 8:
        rows //= 2
        first, second = count[:rows], count[rows:]
        p2, w2 = packed[rows:], weight[rows:]
        for bit in range(7):
            step = 1 << bit
            far = (first & step) != 0
            p2 = jnp.where(far, pltpu.roll(p2, step, 1), p2)
            w2 = jnp.where(far, pltpu.roll(w2, step, 1), w2)
        own = lanes_of(first.shape) < first
        packed = jnp.where(own, packed[:rows], p2)
        weight = jnp.where(own, weight[:rows], w2)
        count = first + second
    return packed, weight, count


def pick_kernel(n_var, kcells, cells_ref, weights_ref, ens_ref, g_ref,
                ens_v, xt, graw, id_v, place_v, w_v, n_v, list_s, n_s, ens_sem, list_sem):
    members, span = ens_ref.shape
    batch_rows = cells_ref.shape[0] // NBATCH
    parts = n_var // 8
    part_rows = batch_rows // parts
    rays_here = batch_rows * LANES // kcells // n_var
    load = pltpu.make_async_copy(ens_ref, ens_v, ens_sem)
    load.start()
    base = lax.axis_index("var") * span
    for part in range(parts):
        packs, weights = [], []
        for batch in range(NBATCH):
            rows = pl.ds(batch * batch_rows + part * part_rows, part_rows)
            place = cells_ref[rows, :] - base
            inside = (place >= 0) & (place < span)
            row = lax.broadcasted_iota(jnp.int32, place.shape, 0)
            ray = batch * rays_here + (row >> 3) * (LANES // kcells) + lanes_of(place.shape) // kcells
            packs.append(jnp.where(inside, jnp.bitwise_or(ray << 16, place & 0xFFFF), -1))
            weights.append(weights_ref[rows, :])
        packed = jnp.concatenate(packs, axis=0)
        packed, weight, count = squeeze_rows(packed, jnp.concatenate(weights, axis=0), packed >= 0)
        valid = lanes_of(count.shape) < count
        out_rows = pl.ds(part * 8, 8)
        place_v[out_rows, :] = jnp.where(valid, packed & 0xFFFF, 0)
        id_v[out_rows, :] = jnp.where(valid, packed >> 16, -1)
        w_v[out_rows, :] = jnp.where(valid, weight, 0.0)
        n_v[out_rows, :] = count
    to_list = pltpu.make_async_copy(place_v, list_s, list_sem.at[0])
    to_count = pltpu.make_async_copy(n_v, n_s, list_sem.at[1])
    to_list.start()
    to_count.start()
    load.wait()
    blank = jnp.zeros((32 - members, LANES), F32)

    def turn(step, carry):
        for group in range(4):
            tiles = []
            for part in range(4):
                at = pl.ds(pl.multiple_of(((step * 4 + group) * 4 + part) * LANES, LANES), LANES)
                tiles += [ens_v[:, at], blank]
            to = pl.ds(pl.multiple_of((step * 4 + group) * LANES, LANES), LANES)
            xt[to, :] = jnp.concatenate(tiles, axis=0).T
        return carry

    lax.fori_loop(0, span // (16 * LANES), turn, 0)
    to_list.wait()
    to_count.wait()

    def gather_row(row, carry):
        def gather_some(block, inner):
            found = []
            for unit in range(16):
                place = list_s[row, block * 16 + unit]
                source = ((place >> 9) << 7) | (place & 127)
                found.append(xt[pl.ds(source, 1), :])
            for unit in range(16):
                graw[pl.ds(row * LANES + block * 16 + unit, 1), :] = found[unit]
            return inner

        lax.fori_loop(0, (jnp.minimum(n_s[row, 0], LANES) + 15) // 16, gather_some, 0)
        return carry

    lax.fori_loop(0, n_var, gather_row, 0)
    sub = lax.broadcasted_iota(jnp.int32, (24, LANES), 0)
    for row in range(n_var):
        raw = graw[pl.ds(row * LANES, LANES), :].T
        place = place_v[pl.ds(row, 1), :]
        ids = id_v[pl.ds(row, 1), :]
        quarter = (place >> 7) & 3
        total = jnp.zeros((24, LANES), F32)
        for piece in range(4):
            total = jnp.where(quarter == piece, raw[32 * piece:32 * piece + 24, :], total)
        total = jnp.where(ids >= 0, total, 0.0) * w_v[pl.ds(row, 1), :]
        total = jnp.where(sub == members, ids.astype(F32), total)
        g_ref[row] = jnp.where(sub == members + 1, place.astype(F32), total)


def pick(ensemble, cell_rows, weight_rows, n_var, kcells):
    members, span = ensemble.shape
    vmem = pl.BlockSpec(memory_space=pltpu.VMEM)
    return pl.pallas_call(
        functools.partial(pick_kernel, n_var, kcells),
        out_shape=jax.ShapeDtypeStruct((n_var, 24, LANES), F32),
        in_specs=[vmem, vmem, pl.BlockSpec(memory_space=pl.ANY)],
        out_specs=vmem,
        scratch_shapes=[
            pltpu.VMEM((members, span), F32),
            pltpu.VMEM((span // 4, LANES), F32),
            pltpu.VMEM((n_var * LANES, LANES), F32),
            pltpu.VMEM((n_var, LANES), jnp.int32),
            pltpu.VMEM((n_var, LANES), jnp.int32),
            pltpu.VMEM((n_var, LANES), F32),
            pltpu.VMEM((n_var, LANES), jnp.int32),
            pltpu.SMEM((n_var, LANES), jnp.int32),
            pltpu.SMEM((n_var, LANES), jnp.int32),
            pltpu.SemaphoreType.DMA,
            pltpu.SemaphoreType.DMA((2,)),
        ],
        compiler_params=pltpu.CompilerParams(vmem_limit_bytes=48 << 20),
        name="pick",
    )(cell_rows, weight_rows, ensemble)


def high_dot(a, b):
    return jnp.dot(a, b, precision=HIGHEST_PREC, preferred_element_type=F32)


def split(x):
    high = x.astype(BF16)
    return high, (x - high.astype(F32)).astype(BF16)


def split_dot(a, b):
    a_high, a_low = split(a)
    b_high, b_low = split(b)
    total = jnp.dot(a_high, b_low, preferred_element_type=F32)
    total = total + jnp.dot(a_low, b_high, preferred_element_type=F32)
    return total + jnp.dot(a_high, b_high, preferred_element_type=F32)


def main_kernel(dims, ens_ref, g_ref, par_ref, out_ref,
                xf, res, xr, state, xb, agb, inc_v, reg_v, dpoly, dhi, dlo,
                mini_s, mini_r, fwd_s, fwd_r, own_sem, red_s, red_r, back_s, back_r):
    n_var, n_mem, members, cells, nobs, n_chunk = dims
    group = members // n_mem
    wide = 24 * n_mem
    sources = n_var // n_mem
    width = cells // n_chunk
    rays_here = nobs // n_var
    p, q = lax.axis_index("var"), lax.axis_index("mem")
    taker = p // sources
    stays = taker == q

    def var_peer(k):
        return {"var": lax.rem(p + k, n_var)}

    def mem_peer(k):
        return {"mem": lax.rem(q + k, n_mem)}

    barrier = pltpu.get_barrier_semaphore()

    def greet(k, carry):
        pl.semaphore_signal(barrier, inc=1, device_id=var_peer(k), device_id_type=MESH)
        return carry

    def greet_sender(k, carry):
        source, part = q * sources + k // n_mem, lax.rem(k, n_mem)

        @pl.when((source != p) | (part != q))
        def _():
            pl.semaphore_signal(barrier, inc=1, device_id={"var": source, "mem": part}, device_id_type=MESH)

        return carry

    lax.fori_loop(0, n_var, greet_sender, 0)
    for k in range(1, n_mem):
        pl.semaphore_signal(barrier, inc=1, device_id=mem_peer(k), device_id_type=MESH)
    lax.fori_loop(1, n_var, greet, 0)
    lane = lanes_of((1, LANES))
    real_lane = (lax.rem(lane, 24) < group) & (lane < wide)
    block = p * n_mem + q
    pl.semaphore_wait(barrier, n_var - 1 + n_mem - 1 + n_var - stays.astype(jnp.int32))

    def send_mini(k, carry):
        there = lax.rem(p + k, n_var)

        @pl.when((k > 0) | jnp.logical_not(stays))
        def _():
            pltpu.make_async_remote_copy(
                src_ref=g_ref.at[there], dst_ref=xr.at[q, lax.rem(p, sources)],
                send_sem=mini_s, recv_sem=mini_r,
                device_id={"var": there, "mem": taker}, device_id_type=MESH).start()

        return carry

    lax.fori_loop(0, n_var, send_mini, 0)

    @pl.when(stays)
    def _():
        xr[q, lax.rem(p, sources)] = g_ref[p]

    def forward(k, chunk):
        there = lax.rem(q + k, n_mem)
        return pltpu.make_async_remote_copy(
            src_ref=ens_ref.at[:, pl.ds(pl.multiple_of(there * cells + chunk * width, LANES), width)],
            dst_ref=xf.at[q, :, pl.ds(pl.multiple_of(chunk * width, LANES), width)],
            send_sem=fwd_s.at[k, chunk], recv_sem=fwd_r.at[k, chunk],
            device_id=mem_peer(k), device_id_type=MESH)

    def start_forward(chunk, carry):
        for k in (2, 1, 3):
            forward(k, chunk).start()
        return carry

    paced = [0]

    def pace(count):
        until = min(paced[0] + count, n_chunk)
        lax.fori_loop(paced[0], until, start_forward, 0)
        paced[0] = until

    pace(PACE[0])
    own = pltpu.make_async_copy(ens_ref.at[:, pl.ds(pl.multiple_of(q * cells, LANES), cells)], xf.at[q], own_sem.at[0])
    own.start()

    def wait_mini(count):
        landed = g_ref.at[pl.ds(0, count)]
        pltpu.make_async_remote_copy(
            src_ref=landed, dst_ref=landed, send_sem=mini_s, recv_sem=mini_r,
            device_id=mem_peer(1), device_id_type=MESH).wait()

    @pl.when(stays)
    def _():
        wait_mini(n_var - 1)

    @pl.when(jnp.logical_not(stays))
    def _():
        wait_mini(n_var)

    sub = lax.broadcasted_iota(jnp.int32, (24, LANES), 0)
    ids, places = [], []
    for source in range(sources):
        for part in range(n_mem):
            tile = xr[part, source]
            state[pl.ds(part * 24, 24), pl.ds(source * LANES, LANES)] = jnp.where(sub < group, tile, 0.0)
        ids.append(xr[0, source, group:group + 1, :])
        places.append(xr[0, source, group + 1:group + 2, :] + ((q * sources + source) * (n_mem * cells)).astype(F32))
    id_row = jnp.concatenate(ids, axis=1)
    scale = 1.0 / (LRAD * cells)
    place_row = jnp.concatenate(places, axis=1) * scale
    own_ray = lax.broadcasted_iota(jnp.int32, (rays_here, 1), 0).astype(F32)

    def own_rows():
        return pl.ds(pl.multiple_of(p * rays_here, rays_here), rays_here)

    def across(batch, k):
        return pltpu.make_async_remote_copy(
            src_ref=xb.at[batch, q], dst_ref=xb.at[batch, q],
            send_sem=red_s.at[batch, k], recv_sem=red_r.at[batch, k],
            device_id=mem_peer(k), device_id_type=MESH)

    def start_reduce(batch):
        chosen = (id_row == own_ray + batch * rays_here).astype(BF16)
        held = state[...]
        high = held.astype(BF16)
        rest = held - high.astype(F32)
        middle = rest.astype(BF16)
        low = (rest - middle.astype(F32)).astype(BF16)
        total = jnp.zeros((rays_here, wide), F32)
        for piece in (low, middle, high):
            total = total + lax.dot_general(chosen, piece, (((1,), (1,)), ((), ())), preferred_element_type=F32)
        xb[batch, q] = jnp.concatenate([total, jnp.zeros((rays_here, LANES - wide), F32)], axis=1)
        for k in (2, 1, 3):
            across(batch, k).start()

    def finish_reduce(batch):
        for k in (2, 1, 3):
            across(batch, k).wait()
        agb[batch, own_rows(), :] = jnp.sum(xb[batch], axis=0)
        mine = agb.at[batch, own_rows()]

        def send(k, carry):
            pltpu.make_async_remote_copy(
                src_ref=mine, dst_ref=mine,
                send_sem=red_s.at[batch, n_mem], recv_sem=red_r.at[batch, n_mem],
                device_id=var_peer(k), device_id_type=MESH).start()
            return carry

        lax.fori_loop(1, n_var, send, 0)
        pace(PACE[2])
        landed = agb.at[batch, pl.ds(0, nobs - rays_here)]
        pltpu.make_async_remote_copy(
            src_ref=landed, dst_ref=landed, send_sem=red_s.at[batch, n_mem], recv_sem=red_r.at[batch, n_mem],
            device_id=var_peer(1), device_id_type=MESH).wait()

    def innovate(batch):
        prior = agb[batch]
        obs = par_ref[:, NBATCH + batch:NBATCH + batch + 1]
        error_var = par_ref[:, 2 * NBATCH + batch:2 * NBATCH + batch + 1]
        mean = jnp.sum(prior, axis=1, keepdims=True) / members
        anomaly = jnp.where(real_lane, prior - mean, 0.0)
        variance = jnp.sum(anomaly * anomaly, axis=1, keepdims=True) / (members - 1) + EPSILON
        total_var = variance + error_var
        post_mean = (mean * error_var + obs * variance) / total_var
        shrink = jnp.sqrt(error_var / total_var)
        increments = jnp.where(real_lane, post_mean - mean + (shrink - 1.0) * anomaly, 0.0)
        inc_v[...] = increments.T
        reg_v[...] = anomaly / ((members - 1) * variance)

    def taper_at(batch, scaled):
        return 1.0 - jnp.abs(scaled - (par_ref[:, batch:batch + 1] + 0.5) * (cells * scale))

    def update_state(batch):
        slopes = split_dot(reg_v[:, 0:wide], state[...])
        slopes = slopes * jnp.maximum(taper_at(batch, place_row), 0.0)
        state[...] += split_dot(inc_v[0:wide, :], slopes)

    def compose(batch):
        for half in range(2):
            start = (block * cells + half * (cells // 2)).astype(F32) * scale
            near, far = taper_at(batch, start), taper_at(batch, start + (cells // 2) * scale)
            inside = near + far > 0.0
            alpha = jnp.where(inside, near, 0.0)
            beta = jnp.where(inside, far - near, 0.0)
            regress = reg_v[...]
            both = jnp.concatenate([regress * alpha, regress * beta], axis=1)
            ab = high_dot(inc_v[0:wide, :], both)
            a, b = ab[:, :LANES], ab[:, LANES:]
            if batch == 0:
                dpoly[half, 0], dpoly[half, 1] = a, b
                continue
            old = jnp.concatenate([dpoly[half, k] for k in range(batch + 1)], axis=1)
            left = jnp.concatenate([a[:, 0:wide], b[:, 0:wide]], axis=0)
            made = high_dot(left, old)
            for k in range(batch + 2):
                total = a if k == 0 else b if k == 1 else jnp.zeros_like(a)
                if k <= batch:
                    total = total + dpoly[half, k] + made[:wide, k * LANES:(k + 1) * LANES]
                if k >= 1:
                    total = total + made[wide:, (k - 1) * LANES:k * LANES]
                dpoly[half, k] = total

    start_reduce(0)
    for batch in range(NBATCH):
        pace(PACE[1])
        if batch:
            compose(batch - 1)
        finish_reduce(batch)
        innovate(batch)
        if batch + 1 < NBATCH:
            update_state(batch)
            start_reduce(batch + 1)
    pace(n_chunk)
    compose(NBATCH - 1)

    terms = NBATCH + 1
    for half in range(2):
        for k in range(terms):
            high, low = split(dpoly[half, k][:, 0:wide])
            dhi[half, pl.ds(k * wide, wide), :] = high
            dlo[half, pl.ds(k * wide, wide), :] = low

    own.wait()

    def back(k, chunk):
        there = lax.rem(q + k, n_mem)
        return pltpu.make_async_remote_copy(
            src_ref=res.at[there, :, pl.ds(pl.multiple_of(chunk * width, LANES), width)],
            dst_ref=out_ref.at[:, pl.ds(pl.multiple_of(q * cells + chunk * width, LANES), width)],
            send_sem=back_s.at[k], recv_sem=back_r.at[k],
            device_id=mem_peer(k), device_id_type=MESH)

    pad = jnp.zeros((24 - group, width), F32)

    def apply(chunk, carry):
        for k in (2, 1, 3):
            forward(k, chunk).wait()
        half = chunk // (n_chunk // 2)
        at = pl.ds(pl.multiple_of(chunk * width, LANES), width)
        pieces = []
        for i in range(n_mem):
            pieces += [xf[i, :, at], pad]
        x = jnp.concatenate(pieces, axis=0)
        high, low = split(x)
        big, small = dhi[half], dlo[half]
        y = jnp.dot(big, high, preferred_element_type=F32)
        y = y + jnp.dot(big, low, preferred_element_type=F32)
        y = y + jnp.dot(small, high, preferred_element_type=F32)
        t = (lanes_of((1, width)) + (chunk - half * (n_chunk // 2)) * width).astype(F32) * (2.0 / cells)
        total = y[(terms - 1) * wide:]
        for k in range(terms - 2, -1, -1):
            total = y[k * wide:(k + 1) * wide] + t * total
        total = x + total
        for i in range(n_mem):
            res[i, :, at] = total[24 * i:24 * i + group]
        for k in (2, 1, 3):
            back(k, chunk).start()
        return carry

    lax.fori_loop(0, n_chunk, apply, 0)
    mine = pl.ds(pl.multiple_of(q * cells, LANES), cells)
    keep = pltpu.make_async_copy(res.at[q], out_ref.at[:, mine], own_sem.at[1])
    keep.start()
    for k in range(1, n_mem):
        source = lax.rem(q + n_mem - k, n_mem)
        landed = out_ref.at[:, pl.ds(pl.multiple_of(source * cells, LANES), cells)]
        pltpu.make_async_remote_copy(
            src_ref=res.at[lax.rem(q + k, n_mem)], dst_ref=landed, send_sem=back_s.at[k], recv_sem=back_r.at[k],
            device_id=mem_peer(k), device_id_type=MESH).wait()
    keep.wait()


def assimilate(ensemble, picked, params, n_var, n_mem):
    group, span = ensemble.shape
    cells = span // n_mem
    nobs = params.shape[0]
    wide = 24 * n_mem
    slots = n_var // n_mem * LANES
    rays_here = nobs // n_var
    vmem = pl.BlockSpec(memory_space=pltpu.VMEM)
    anywhere = pl.BlockSpec(memory_space=pl.ANY)
    dma = pltpu.SemaphoreType.DMA
    dims = (n_var, n_mem, group * n_mem, cells, nobs, N_CHUNK)
    return pl.pallas_call(
        functools.partial(main_kernel, dims),
        out_shape=jax.ShapeDtypeStruct((group, span), F32),
        in_specs=[anywhere, vmem, vmem],
        out_specs=anywhere,
        scratch_shapes=[
            pltpu.VMEM((n_mem, group, cells), F32),
            pltpu.VMEM((n_mem, group, cells), F32),
            pltpu.VMEM((n_mem, n_var // n_mem, 24, LANES), F32),
            pltpu.VMEM((wide, slots), F32),
            pltpu.VMEM((NBATCH, n_mem, rays_here, LANES), F32),
            pltpu.VMEM((NBATCH, nobs, LANES), F32),
            pltpu.VMEM((LANES, nobs), F32),
            pltpu.VMEM((nobs, LANES), F32),
            pltpu.VMEM((2, NBATCH + 1, wide, LANES), F32),
            pltpu.VMEM((2, (NBATCH + 1) * wide, wide), BF16),
            pltpu.VMEM((2, (NBATCH + 1) * wide, wide), BF16),
            dma, dma,
            dma((n_mem, N_CHUNK)), dma((n_mem, N_CHUNK)),
            dma((2,)),
            dma((NBATCH, n_mem + 1)), dma((NBATCH, n_mem + 1)),
            dma((n_mem,)), dma((n_mem,)),
        ],
        compiler_params=pltpu.CompilerParams(collective_id=1, has_side_effects=True, vmem_limit_bytes=48 << 20),
        name="assimilate",
    )(ensemble, picked, params)


def owner_order(rays, n_var, per_row):
    count = rays.shape[-1] // n_var
    return rays.reshape(-1, n_var // 8, count // per_row, 8, per_row).transpose(0, 1, 3, 2, 4).reshape(rays.shape)


def fast(ensemble, cell_rows, weight_rows, ray_centers, obs_values, obs_var):
    n_var, n_mem = lax.axis_size("var"), lax.axis_size("mem")
    nobs = ray_centers.shape[1]
    kcells = cell_rows.size // (NBATCH * nobs)
    picked = pick(ensemble, cell_rows, weight_rows, n_var, kcells)
    params = jnp.concatenate([ray_centers.astype(F32), obs_values, obs_var], axis=0)
    params = owner_order(params, n_var, LANES // kcells).T
    return assimilate(ensemble, picked, params, n_var, n_mem)


def slow(ensemble, cell_rows, weight_rows, ray_centers, obs_values, obs_var):
    shape = (*ray_centers.shape, cell_rows.size // ray_centers.size)
    return plain(ensemble, cell_rows.reshape(shape), weight_rows.reshape(shape), ray_centers, obs_values, obs_var)


def fits(cell_rows, span, n_var):
    home = cell_rows.reshape(NBATCH, n_var // 8, -1, 8, LANES) // span
    hits = home[..., None] == jnp.arange(n_var, dtype=jnp.int32)
    return jnp.max(jnp.sum(hits.astype(jnp.int32), axis=(0, 2, 4))) <= LANES


def shards(ensemble, ray_cells, ray_weights, *rest):
    cell_rows, weight_rows = ray_cells.reshape(-1, LANES), ray_weights.reshape(-1, LANES)
    room = fits(cell_rows, ensemble.shape[1], lax.axis_size("var"))
    return lax.cond(room, fast, slow, ensemble, cell_rows, weight_rows, *rest)


def solution(mesh):
    placed = (P("mem", "var"), P(), P(), P(), P(), P())
    return jax.shard_map(
        shards, mesh=mesh, in_specs=placed, out_specs=P("mem", "var"), check_vma=False
    )
```

time: 267 us -> 201 us (0.75)
  Pallas kernels: 239 us -> 186 us
  between operations: 14.1 us -> 0.69 us
    pallas_call x1, Pallas kernels: 210 us -> 167 us  [assimilate(): pl.pallas_call(functools.partial(main_kernel, dims), out_shape=jax.ShapeD...]
    pallas_call x1, Pallas kernels: 28.1 us -> 19.3 us  [pick(): pl.pallas_call(functools.partial(pick_kernel, n_var, kcells), out_shape=j...]
where the time goes in v2:
time: 201 us; the launch traced here: 200 us
  Pallas kernels  186 us (93%)
  local copies, waits for them, and re-layouts  9.91 us (5%)
  other arithmetic  3.34 us (2%)
    pallas_call x1, Pallas kernels, assimilate(): pl.pallas_call(functools.partial(main_kernel, dims), out_shape=jax.ShapeD...  167 us
    pallas_call x1, Pallas kernels, pick(): pl.pallas_call(functools.partial(pick_kernel, n_var, kcells), out_shape=j...  19.3 us
    unnamed x2, local copies, waits for them, and re-layouts  7.03 us

profile of v2, /device:TPU:1, one launch (start us, length us, event | category | flops | bytes accessed | tf_op | source)
XLA Modules:
  0.0 200.5 jit_solution(3137154630155531514)
XLA Ops:
  0.0 1.1 copy.87
  1.2 0.1 reshape_reshape.3
  1.3 0.1 add_select_fusion
  1.5 1.2 convert_reduce_fusion
  2.6 0.6 reduce_max.9
  3.9 190.7 %conditional.1 = (f32[20,65536]{1,0:T(8,128)}) conditional(s32[]{:T(128)} %convert_element_type.49, (f32[20,65536]{1,0:T(8,128)}, s32[4,256,64]{1,2,0:T(8,128)}, f32[4,256,64]{1,2,0:T(8,128)}, f32[4,256]{1,0:T(4,128)}, f32[4,256]{1,0:T(4,128)}, /*index=5*/s32[4,256]{1,0:T(4,128)}) %tuple.12, (s32[4,256,64]{1,2,0:T(8,128)}, ...), branch_computations={%region_2.16_spmd, %region_15.17_spmd} | conditional | flops 32388296704 | bytes 523480768 | solution.py:576
  4.1 0.7 convert_element_type.45
  4.8 0.7 pad_maximum_fusion
  5.5 0.1 copy.75
  5.7 1.1 copy.91
  6.9 0.1 reshape.431.weights_ref
  7.0 1.1 copy.90
  8.2 0.1 reshape.430.cells_ref
  8.3 0.0 copy-start
  8.3 19.3 %pick.1.g_ref = f32[32,24,128]{2,1,0:T(8,128)S(1)} custom-call(s32[512,128]{1,0:T(8,128)S(1)} %reshape.430.cells_ref, f32[512,128]{1,0:T(8,128)S(1)} %reshape.431.weights_ref, f32[20,65536]{1,0:T(8,128)} %get-tuple-element.41.ens_ref), custom_call_target="tpu_custom_call" | custom-call | tf_op jit(solution)/shard_map/cond/branch_1_fun/pick/pallas_call | solution.py:196
  27.6 0.0 copy-done
  27.6 166.6 %assimilate.1 = f32[20,65536]{1,0:T(8,128)} custom-call(f32[20,65536]{1,0:T(8,128)S(1)} %copy-done, f32[32,24,128]{2,1,0:T(8,128)S(1)} %pick.1.g_ref, f32[256,12]{1,0:T(8,128)S(1)} %bitcast.137), custom_call_target="tpu_custom_call" | custom-call | tf_op jit(solution)/shard_map/cond/branch_1_fun/assimilate/pallas_call | solution.py:519
  194.6 5.9 %copy.108 = f32[20,65536]{1,0:T(8,128)} copy(f32[20,65536]{1,0:T(8,128)} %get-tuple-element.47) | data formatting | bytes 10485760
  (1 shorter events, 0.0 us)
Async XLA Ops:
  8.3 19.3 %copy-start = (f32[20,65536]{1,0:T(8,128)S(1)}, f32[20,65536]{1,0:T(8,128)}, u32[]{:S(2)}) copy-start(f32[20,65536]{1,0:T(8,128)} %get-tuple-element.41.ens_ref) | copy-start | bytes 15728644 | tf_op jit(solution)/shard_map/cond

commit v3 on v2

--- a/solution.py
+++ b/solution.py
@@ -15,7 +15,8 @@
 HIGHEST_PREC = lax.Precision.HIGHEST
 MESH = pl.DeviceIdType.MESH
 N_CHUNK = 16
-PACE = (2, 1, 2)
+EARLY = 6
+PACE = (2, 1, 1, 0)
 BF16 = jnp.bfloat16
 F32 = jnp.float32
 
@@ -112,35 +113,40 @@
     return packed, weight, count
 
 
-def pick_kernel(n_var, kcells, cells_ref, weights_ref, ens_ref, g_ref,
-                ens_v, xt, graw, id_v, place_v, w_v, n_v, list_s, n_s, ens_sem, list_sem):
+def pick_kernel(n_var, cells_in, weights_in, ens_ref, g_ref,
+                cells_ref, weights_ref, ens_v, xt, graw, id_v, place_v, from_v, w_v, n_v, list_s, n_s, ens_sem, list_sem):
     members, span = ens_ref.shape
-    batch_rows = cells_ref.shape[0] // NBATCH
-    parts = n_var // 8
-    part_rows = batch_rows // parts
-    rays_here = batch_rows * LANES // kcells // n_var
+    nobs, kcells = cells_ref.shape[1:]
+    rays_here = nobs // n_var
     load = pltpu.make_async_copy(ens_ref, ens_v, ens_sem)
     load.start()
+    for batch in range(NBATCH):
+        cells_ref[batch] = cells_in[batch].T
+        weights_ref[batch] = weights_in[batch].T
     base = lax.axis_index("var") * span
-    for part in range(parts):
+    fold = LANES // kcells
+    steps = rays_here // fold
+    for part in range(n_var // 8):
         packs, weights = [], []
         for batch in range(NBATCH):
-            rows = pl.ds(batch * batch_rows + part * part_rows, part_rows)
-            place = cells_ref[rows, :] - base
-            inside = (place >= 0) & (place < span)
-            row = lax.broadcasted_iota(jnp.int32, place.shape, 0)
-            ray = batch * rays_here + (row >> 3) * (LANES // kcells) + lanes_of(place.shape) // kcells
-            packs.append(jnp.where(inside, jnp.bitwise_or(ray << 16, place & 0xFFFF), -1))
-            weights.append(weights_ref[rows, :])
+            for step in range(steps):
+                rows = [pl.ds(part * 8 * rays_here + step + side * steps, 8, stride=rays_here) for side in range(fold)]
+                place = jnp.concatenate([cells_ref[batch, row, :] for row in rows], axis=1) - base
+                inside = (place >= 0) & (place < span)
+                ray = batch * rays_here + step + lanes_of(place.shape) // kcells * steps
+                packs.append(jnp.where(inside, jnp.bitwise_or(ray << 16, place & 0xFFFF), -1))
+                weights.append(jnp.concatenate([weights_ref[batch, row, :] for row in rows], axis=1))
         packed = jnp.concatenate(packs, axis=0)
         packed, weight, count = squeeze_rows(packed, jnp.concatenate(weights, axis=0), packed >= 0)
         valid = lanes_of(count.shape) < count
         out_rows = pl.ds(part * 8, 8)
-        place_v[out_rows, :] = jnp.where(valid, packed & 0xFFFF, 0)
+        place = jnp.where(valid, packed & 0xFFFF, 0)
+        place_v[out_rows, :] = place
+        from_v[out_rows, :] = ((place >> 9) << 7) | (place & 127)
         id_v[out_rows, :] = jnp.where(valid, packed >> 16, -1)
         w_v[out_rows, :] = jnp.where(valid, weight, 0.0)
         n_v[out_rows, :] = count
-    to_list = pltpu.make_async_copy(place_v, list_s, list_sem.at[0])
+    to_list = pltpu.make_async_copy(from_v, list_s, list_sem.at[0])
     to_count = pltpu.make_async_copy(n_v, n_s, list_sem.at[1])
     to_list.start()
     to_count.start()
@@ -165,9 +171,7 @@
         def gather_some(block, inner):
             found = []
             for unit in range(16):
-                place = list_s[row, block * 16 + unit]
-                source = ((place >> 9) << 7) | (place & 127)
-                found.append(xt[pl.ds(source, 1), :])
+                found.append(xt[pl.ds(list_s[row, block * 16 + unit], 1), :])
             for unit in range(16):
                 graw[pl.ds(row * LANES + block * 16 + unit, 1), :] = found[unit]
             return inner
@@ -190,18 +194,21 @@
         g_ref[row] = jnp.where(sub == members + 1, place.astype(F32), total)
 
 
-def pick(ensemble, cell_rows, weight_rows, n_var, kcells):
+def pick(ensemble, ray_cells, ray_weights, n_var):
     members, span = ensemble.shape
     vmem = pl.BlockSpec(memory_space=pltpu.VMEM)
     return pl.pallas_call(
-        functools.partial(pick_kernel, n_var, kcells),
+        functools.partial(pick_kernel, n_var),
         out_shape=jax.ShapeDtypeStruct((n_var, 24, LANES), F32),
         in_specs=[vmem, vmem, pl.BlockSpec(memory_space=pl.ANY)],
         out_specs=vmem,
         scratch_shapes=[
+            pltpu.VMEM(ray_cells.shape, jnp.int32),
+            pltpu.VMEM(ray_cells.shape, F32),
             pltpu.VMEM((members, span), F32),
             pltpu.VMEM((span // 4, LANES), F32),
             pltpu.VMEM((n_var * LANES, LANES), F32),
+            pltpu.VMEM((n_var, LANES), jnp.int32),
             pltpu.VMEM((n_var, LANES), jnp.int32),
             pltpu.VMEM((n_var, LANES), jnp.int32),
             pltpu.VMEM((n_var, LANES), F32),
@@ -212,8 +219,9 @@
             pltpu.SemaphoreType.DMA((2,)),
         ],
         compiler_params=pltpu.CompilerParams(vmem_limit_bytes=48 << 20),
+        cost_estimate=pl.CostEstimate(flops=1 << 30, bytes_accessed=64 << 20, transcendentals=0),
         name="pick",
-    )(cell_rows, weight_rows, ensemble)
+    )(ray_cells.transpose(0, 2, 1), ray_weights.transpose(0, 2, 1), ensemble)
 
 
 def high_dot(a, b):
@@ -233,8 +241,8 @@
     return total + jnp.dot(a_high, b_high, preferred_element_type=F32)
 
 
-def main_kernel(dims, ens_ref, g_ref, par_ref, out_ref,
-                xf, res, xr, state, xb, agb, inc_v, reg_v, dpoly, dhi, dlo,
+def main_kernel(dims, ens_ref, g_ref, centers_ref, obs_ref, var_ref, early_refs, out_ref,
+                par_ref, xf, res, xr, state, xb, agb, inc_v, reg_v, dpoly, dhi, dlo,
                 mini_s, mini_r, fwd_s, fwd_r, own_sem, red_s, red_r, back_s, back_r):
     n_var, n_mem, members, cells, nobs, n_chunk = dims
     group = members // n_mem
@@ -243,8 +251,8 @@
     width = cells // n_chunk
     rays_here = nobs // n_var
     p, q = lax.axis_index("var"), lax.axis_index("mem")
-    taker = p // sources
-    stays = taker == q
+    first = lax.rem(q + n_mem - p // sources, n_mem) * sources
+    stays = p // sources == first // sources
 
     def var_peer(k):
         return {"var": lax.rem(p + k, n_var)}
@@ -259,7 +267,7 @@
         return carry
 
     def greet_sender(k, carry):
-        source, part = q * sources + k // n_mem, lax.rem(k, n_mem)
+        source, part = first + k // n_mem, lax.rem(k, n_mem)
 
         @pl.when((source != p) | (part != q))
         def _():
@@ -274,10 +282,14 @@
     lane = lanes_of((1, LANES))
     real_lane = (lax.rem(lane, 24) < group) & (lane < wide)
     block = p * n_mem + q
+    rows = [centers_ref[...].astype(F32), obs_ref[...], var_ref[...]]
+    rows.append(jnp.zeros((LANES - 3 * NBATCH, nobs), F32))
+    par_ref[...] = jnp.concatenate(rows, axis=0).T
     pl.semaphore_wait(barrier, n_var - 1 + n_mem - 1 + n_var - stays.astype(jnp.int32))
 
     def send_mini(k, carry):
         there = lax.rem(p + k, n_var)
+        taker = lax.rem(p // sources + there // sources, n_mem)
 
         @pl.when((k > 0) | jnp.logical_not(stays))
         def _():
@@ -307,7 +319,7 @@
             forward(k, chunk).start()
         return carry
 
-    paced = [0]
+    paced = [EARLY]
 
     def pace(count):
         until = min(paced[0] + count, n_chunk)
@@ -317,6 +329,11 @@
     pace(PACE[0])
     own = pltpu.make_async_copy(ens_ref.at[:, pl.ds(pl.multiple_of(q * cells, LANES), cells)], xf.at[q], own_sem.at[0])
     own.start()
+    landing = []
+    for k in range(1, n_mem):
+        there = xf.at[lax.rem(q + n_mem - k, n_mem), :, pl.ds(0, EARLY * width)]
+        landing.append(pltpu.make_async_copy(early_refs[k - 1], there, own_sem.at[1 + k]))
+        landing[-1].start()
 
     def wait_mini(count):
         landed = g_ref.at[pl.ds(0, count)]
@@ -339,7 +356,7 @@
             tile = xr[part, source]
             state[pl.ds(part * 24, 24), pl.ds(source * LANES, LANES)] = jnp.where(sub < group, tile, 0.0)
         ids.append(xr[0, source, group:group + 1, :])
-        places.append(xr[0, source, group + 1:group + 2, :] + ((q * sources + source) * (n_mem * cells)).astype(F32))
+        places.append(xr[0, source, group + 1:group + 2, :] + ((first + source) * (n_mem * cells)).astype(F32))
     id_row = jnp.concatenate(ids, axis=1)
     scale = 1.0 / (LRAD * cells)
     place_row = jnp.concatenate(places, axis=1) * scale
@@ -441,6 +458,7 @@
         if batch:
             compose(batch - 1)
         finish_reduce(batch)
+        pace(PACE[3])
         innovate(batch)
         if batch + 1 < NBATCH:
             update_state(batch)
@@ -456,6 +474,8 @@
             dlo[half, pl.ds(k * wide, wide), :] = low
 
     own.wait()
+    for copy in landing:
+        copy.wait()
 
     def back(k, chunk):
         there = lax.rem(q + k, n_mem)
@@ -468,8 +488,11 @@
     pad = jnp.zeros((24 - group, width), F32)
 
     def apply(chunk, carry):
-        for k in (2, 1, 3):
-            forward(k, chunk).wait()
+        @pl.when(chunk >= EARLY)
+        def _():
+            for k in (2, 1, 3):
+                forward(k, chunk).wait()
+
         half = chunk // (n_chunk // 2)
         at = pl.ds(pl.multiple_of(chunk * width, LANES), width)
         pieces = []
@@ -490,12 +513,13 @@
             res[i, :, at] = total[24 * i:24 * i + group]
         for k in (2, 1, 3):
             back(k, chunk).start()
+        home = pl.ds(pl.multiple_of(q * cells + chunk * width, LANES), width)
+        pltpu.make_async_copy(res.at[q, :, at], out_ref.at[:, home], own_sem.at[1]).start()
         return carry
 
     lax.fori_loop(0, n_chunk, apply, 0)
     mine = pl.ds(pl.multiple_of(q * cells, LANES), cells)
     keep = pltpu.make_async_copy(res.at[q], out_ref.at[:, mine], own_sem.at[1])
-    keep.start()
     for k in range(1, n_mem):
         source = lax.rem(q + n_mem - k, n_mem)
         landed = out_ref.at[:, pl.ds(pl.multiple_of(source * cells, LANES), cells)]
@@ -505,10 +529,10 @@
     keep.wait()
 
 
-def assimilate(ensemble, picked, params, n_var, n_mem):
+def assimilate(ensemble, picked, ray_centers, obs_values, obs_var, early, n_var, n_mem):
     group, span = ensemble.shape
     cells = span // n_mem
-    nobs = params.shape[0]
+    nobs = ray_centers.shape[1]
     wide = 24 * n_mem
     slots = n_var // n_mem * LANES
     rays_here = nobs // n_var
@@ -519,9 +543,10 @@
     return pl.pallas_call(
         functools.partial(main_kernel, dims),
         out_shape=jax.ShapeDtypeStruct((group, span), F32),
-        in_specs=[anywhere, vmem, vmem],
+        in_specs=[anywhere, vmem, vmem, vmem, vmem, [anywhere] * len(early)],
         out_specs=anywhere,
         scratch_shapes=[
+            pltpu.VMEM((nobs, LANES), F32),
             pltpu.VMEM((n_mem, group, cells), F32),
             pltpu.VMEM((n_mem, group, cells), F32),
             pltpu.VMEM((n_mem, n_var // n_mem, 24, LANES), F32),
@@ -535,45 +560,44 @@
             pltpu.VMEM((2, (NBATCH + 1) * wide, wide), BF16),
             dma, dma,
             dma((n_mem, N_CHUNK)), dma((n_mem, N_CHUNK)),
-            dma((2,)),
+            dma((1 + n_mem,)),
             dma((NBATCH, n_mem + 1)), dma((NBATCH, n_mem + 1)),
             dma((n_mem,)), dma((n_mem,)),
         ],
         compiler_params=pltpu.CompilerParams(collective_id=1, has_side_effects=True, vmem_limit_bytes=48 << 20),
         name="assimilate",
-    )(ensemble, picked, params)
-
-
-def owner_order(rays, n_var, per_row):
-    count = rays.shape[-1] // n_var
-    return rays.reshape(-1, n_var // 8, count // per_row, 8, per_row).transpose(0, 1, 3, 2, 4).reshape(rays.shape)
-
-
-def fast(ensemble, cell_rows, weight_rows, ray_centers, obs_values, obs_var):
+    )(ensemble, picked, ray_centers, obs_values, obs_var, early)
+
+
+def first_columns(ensemble, n_mem):
+    group, span = ensemble.shape
+    cells = span // n_mem
+    q = lax.axis_index("mem")
+    arrived = []
+    for k in range(1, n_mem):
+        start = lax.rem(q + k, n_mem) * cells
+        piece = lax.dynamic_slice(ensemble, (0, start), (group, EARLY * (cells // N_CHUNK)))
+        arrived.append(lax.ppermute(piece, "mem", [(i, (i + k) % n_mem) for i in range(n_mem)]))
+    return arrived
+
+
+def fast(ensemble, ray_cells, ray_weights, ray_centers, obs_values, obs_var):
     n_var, n_mem = lax.axis_size("var"), lax.axis_size("mem")
-    nobs = ray_centers.shape[1]
-    kcells = cell_rows.size // (NBATCH * nobs)
-    picked = pick(ensemble, cell_rows, weight_rows, n_var, kcells)
-    params = jnp.concatenate([ray_centers.astype(F32), obs_values, obs_var], axis=0)
-    params = owner_order(params, n_var, LANES // kcells).T
-    return assimilate(ensemble, picked, params, n_var, n_mem)
-
-
-def slow(ensemble, cell_rows, weight_rows, ray_centers, obs_values, obs_var):
-    shape = (*ray_centers.shape, cell_rows.size // ray_centers.size)
-    return plain(ensemble, cell_rows.reshape(shape), weight_rows.reshape(shape), ray_centers, obs_values, obs_var)
-
-
-def fits(cell_rows, span, n_var):
-    home = cell_rows.reshape(NBATCH, n_var // 8, -1, 8, LANES) // span
-    hits = home[..., None] == jnp.arange(n_var, dtype=jnp.int32)
-    return jnp.max(jnp.sum(hits.astype(jnp.int32), axis=(0, 2, 4))) <= LANES
-
-
-def shards(ensemble, ray_cells, ray_weights, *rest):
-    cell_rows, weight_rows = ray_cells.reshape(-1, LANES), ray_weights.reshape(-1, LANES)
-    room = fits(cell_rows, ensemble.shape[1], lax.axis_size("var"))
-    return lax.cond(room, fast, slow, ensemble, cell_rows, weight_rows, *rest)
+    early = first_columns(ensemble, n_mem)
+    picked = pick(ensemble, ray_cells, ray_weights, n_var)
+    return assimilate(ensemble, picked, ray_centers, obs_values, obs_var, early, n_var, n_mem)
+
+
+def fits(ray_cells, span, n_var):
+    home = ray_cells.transpose(0, 2, 1) // span
+    hits = home[:, :, None, :] == jnp.arange(n_var, dtype=jnp.int32)[:, None]
+    by_ray = jnp.sum(hits.astype(jnp.int32), axis=(0, 1))
+    return jnp.max(jnp.sum(by_ray.reshape(n_var, n_var, -1), axis=2)) <= LANES
+
+
+def shards(*arrays):
+    room = fits(arrays[1], arrays[0].shape[1], lax.axis_size("var"))
+    return lax.cond(room, lambda made, *rest: made, lambda made, *rest: plain(*rest), fast(*arrays), *arrays)
 
 
 def solution(mesh):

time: 201 us -> 180 us (0.90)
  Pallas kernels: 186 us -> 158 us
  starting transfers between devices: 0 us -> 4.43 us
  waiting for transfers between devices: 0 us -> 3.28 us
    pallas_call x1, Pallas kernels: 167 us -> 138 us  [assimilate(): pl.pallas_call(functools.partial(main_kernel, dims), out_shape=jax.ShapeD...]
    ppermute x0 -> x3, starting transfers between devices: none -> 4.43 us  [first_columns(): lax.ppermute(piece, 'mem', [(i, (i + k) % n_mem) for i in range(n_mem)])]
    ppermute x0 -> x3, waiting for transfers between devices: none -> 3.28 us  [first_columns(): lax.ppermute(piece, 'mem', [(i, (i + k) % n_mem) for i in range(n_mem)])]
    dynamic_slice x0 -> x1, local copies, waits for them, and re-layouts: none -> 2.43 us  [first_columns(): lax.dynamic_slice(ensemble, (0, start), (group, EARLY * (cells // N_CHUNK)))]
    another operation x3 -> x0, local copies, waits for them, and re-layouts: 2.43 us -> none
    unnamed x2 -> x11, local copies, waits for them, and re-layouts: 7.03 us -> 5.91 us
  transfers between devices with their start and end apart: 0 -> 3, of which waited for: 0 -> 1; matrix products, arithmetic and copies ran while one was open for 0% -> 2% of each run, Pallas kernels for 0% -> 11%
where the time goes in v3:
time: 180 us; the launch traced here: 179 us
  Pallas kernels  158 us (88%)
  local copies, waits for them, and re-layouts  9.1 us (5%)
  starting transfers between devices  4.43 us (2%)
  other arithmetic  3.71 us (2%)
  waiting for transfers between devices  3.28 us (2%)
    pallas_call x1, Pallas kernels, assimilate(): pl.pallas_call(functools.partial(main_kernel, dims), out_shape=jax.ShapeD...  138 us
    pallas_call x1, Pallas kernels, pick(): pl.pallas_call(functools.partial(pick_kernel, n_var), out_shape=jax.Shape...  19.9 us
    unnamed x11, local copies, waits for them, and re-layouts  5.91 us
    ppermute x3, starting transfers between devices, first_columns(): lax.ppermute(piece, 'mem', [(i, (i + k) % n_mem) for i in range(n_mem)])  4.43 us
  transfers between devices with their start and end apart: 3, of which 1 were waited for; matrix products, arithmetic and copies ran while one was open for 2% of the time, Pallas kernels for 11%

profile of v3, /device:TPU:1, one launch (start us, length us, event | category | flops | bytes accessed | tf_op | source)
XLA Modules:
  0.0 179.3 jit_solution(5762678324386635178)
XLA Ops:
  0.0 0.0 copy-start
  0.0 0.0 copy-start.3
  0.0 0.0 copy-start.4
  0.0 0.0 copy-start.2
  0.0 0.0 copy-start.1
  0.1 2.4 %constant_dynamic-slice_fusion = (f32[20,6144]{1,0:T(8,128)}, f32[20,6144]{1,0:T(8,128)S(1)}, f32[20,6144]{1,0:T(8,128)S(1)}) fusion(f32[20,65536]{1,0:T(8,128)} %ens_ref.3, s32[]{:T(128)S(6)} %select_n.49, s32[]{:T(128)S(6)} %select_n.48, s32[]{:T(128)S(6)} %select_n.47), kind=kLoop, calls=%fused_computation.127 | loop fusion | bytes 2949132 | tf_op jit(solution)/shard_map/dynamic_slice | solution.py:579
  2.5 3.3 %collective-permute-start.2 = (f32[20,6144]{1,0:T(8,128)}, f32[20,6144]{1,0:T(8,128)S(1)}, u32[]{:S(2)}, u32[]{:S(2)}) collective-permute-start(f32[20,6144]{1,0:T(8,128)} %get-tuple-element.93), channel_id=1, source_target_pairs={{0,3},{1,0},{2,1},{3,2},{4,7},{5,4},{6,5},{7,6},{8,11},{9,8},{10,9... | collective-permute-start | bytes 1474568 | tf_op jit(solution)/shard_map/ppermute | solution.py:580
  5.8 0.5 collective-permute-start.1
  6.3 0.6 collective-permute-start
  6.9 1.1 add_select_fusion
  8.0 1.0 convert_reduce_fusion
  9.1 0.8 copy.59
  9.8 0.9 bitcast_reduce_fusion.4
  10.8 0.6 reduce_max.9
  12.0 19.9 %pick.1.g_ref = f32[32,24,128]{2,1,0:T(8,128)S(1)} custom-call(s32[4,64,256]{2,1,0:T(8,128)} %bitcast.152, f32[4,64,256]{2,1,0:T(8,128)} %bitcast.159, f32[20,65536]{1,0:T(8,128)} %ens_ref.3), custom_call_target="tpu_custom_call" | custom-call | flops 1073741824 | bytes 67108864 | tf_op jit(solution)/shard_map/pick/pallas_call | solution.py:200
  31.9 0.0 collective-permute-done.2.early_refs_2_
  31.9 0.0 collective-permute-done.1.early_refs_1_
  31.9 3.3 %collective-permute-done.early_refs_0_ = f32[20,6144]{1,0:T(8,128)S(1)} collective-permute-done((f32[20,6144]{1,0:T(8,128)S(1)}, f32[20,6144]{1,0:T(8,128)S(1)}, u32[]{:S(2)}, u32[]{:S(2)}) %collective-permute-start) | collective-permute-done | bytes 491552 | tf_op jit(solution)/shard_map/ppermute | solution.py:580
  35.2 0.0 copy-done
  35.2 0.0 copy-done.3
  35.2 0.0 copy-done.4
  35.2 0.0 copy-done.2
  35.2 0.0 copy-done.1
  35.2 137.9 %assimilate.1 = f32[20,65536]{1,0:T(8,128)} custom-call(f32[20,65536]{1,0:T(8,128)} %ens_ref.3, f32[32,24,128]{2,1,0:T(8,128)S(1)} %pick.1.g_ref, s32[4,256]{1,0:T(4,128)S(1)} %copy-done.2, f32[4,256]{1,0:T(4,128)S(1)} %copy-done.4, f32[4,256]{1,0:T(4,128)S(1)} %copy-done.3, f32[20,6144]{1,0:T(8,128)S(1)} %collective-permute-done.early_refs_0_, ...), custom_call_target="tpu_custom_call" | custom-call | tf_op jit(solution)/shard_map/assimilate/pallas_call | solution.py:543
  173.1 0.3 conditional.1
  173.4 5.9 %copy.78 = f32[20,65536]{1,0:T(8,128)} copy(f32[20,65536]{1,0:T(8,128)} %get-tuple-element.28) | data formatting | bytes 10485760
Async XLA Ops:
  0.0 35.2 %copy-start = (s32[4,256,64]{1,2,0:T(8,128)S(1)}, s32[4,256,64]{1,2,0:T(8,128)}, u32[]{:S(2)}) copy-start(s32[4,256,64]{1,2,0:T(8,128)} %param.11) | copy-start | bytes 786436
  0.0 35.2 %copy-start.3 = (f32[4,256]{1,0:T(4,128)S(1)}, f32[4,256]{1,0:T(4,128)}, u32[]{:S(2)}) copy-start(f32[4,256]{1,0:T(4,128)} %var_ref.1) | copy-start | bytes 12292
  0.0 35.2 %copy-start.4 = (f32[4,256]{1,0:T(4,128)S(1)}, f32[4,256]{1,0:T(4,128)}, u32[]{:S(2)}) copy-start(f32[4,256]{1,0:T(4,128)} %obs_ref.1) | copy-start | bytes 12292
  0.0 35.2 %copy-start.2 = (s32[4,256]{1,0:T(4,128)S(1)}, s32[4,256]{1,0:T(4,128)}, u32[]{:S(2)}) copy-start(s32[4,256]{1,0:T(4,128)} %centers_ref.1) | copy-start | bytes 12292
  0.0 35.2 %copy-start.1 = (f32[4,256,64]{1,2,0:T(8,128)S(1)}, f32[4,256,64]{1,2,0:T(8,128)}, u32[]{:S(2)}) copy-start(f32[4,256,64]{1,2,0:T(8,128)} %param.12) | copy-start | bytes 786436
  2.5 29.4 %collective-permute-start.2 = (f32[20,6144]{1,0:T(8,128)}, f32[20,6144]{1,0:T(8,128)S(1)}, u32[]{:S(2)}, u32[]{:S(2)}) collective-permute-start(f32[20,6144]{1,0:T(8,128)} %get-tuple-element.93), channel_id=1, source_target_pairs={{0,3},{1,0},{2,1},{3,2},{4,7},{5,4},{6,5},{7,6},{8,11},{9,8},{10,9... | collective-permute-start | bytes 1474568 | tf_op jit(solution)/shard_map/ppermute | solution.py:580
  5.8 26.1 %collective-permute-start.1 = (f32[20,6144]{1,0:T(8,128)S(1)}, f32[20,6144]{1,0:T(8,128)S(1)}, u32[]{:S(2)}, u32[]{:S(2)}) collective-permute-start(f32[20,6144]{1,0:T(8,128)S(1)} %get-tuple-element.94), channel_id=1, source_target_pairs={{0,2},{1,3},{2,0},{3,1},{4,6},{5,7},{6,4},{7,5},{8,10},{9,11},{10,... | collective-permute-start | bytes 1474568 | tf_op jit(solution)/shard_map/ppermute | solution.py:580
  6.3 28.9 %collective-permute-start = (f32[20,6144]{1,0:T(8,128)S(1)}, f32[20,6144]{1,0:T(8,128)S(1)}, u32[]{:S(2)}, u32[]{:S(2)}) collective-permute-start(f32[20,6144]{1,0:T(8,128)S(1)} %get-tuple-element.95), channel_id=1, source_target_pairs={{0,1},{1,2},{2,3},{3,0},{4,5},{5,6},{6,7},{7,4},{8,9},{9,10},{10,1... | collective-permute-start | bytes 1474568 | tf_op jit(solution)/shard_map/ppermute | solution.py:580

commit v4 on v3

--- a/solution.py
+++ b/solution.py
@@ -15,8 +15,11 @@
 HIGHEST_PREC = lax.Precision.HIGHEST
 MESH = pl.DeviceIdType.MESH
 N_CHUNK = 16
+TAIL_PARTS = 4
+FULL = 16
+LAG = 3
 EARLY = 6
-PACE = (2, 1, 1, 0)
+PACE = (3, 1, 2, 0)
 BF16 = jnp.bfloat16
 F32 = jnp.float32
 
@@ -113,7 +116,7 @@
     return packed, weight, count
 
 
-def pick_kernel(n_var, cells_in, weights_in, ens_ref, g_ref,
+def pick_kernel(n_var, n_mem, cells_in, weights_in, ens_ref, g_ref, tails_ref,
                 cells_ref, weights_ref, ens_v, xt, graw, id_v, place_v, from_v, w_v, n_v, list_s, n_s, ens_sem, list_sem):
     members, span = ens_ref.shape
     nobs, kcells = cells_ref.shape[1:]
@@ -152,6 +155,18 @@
     to_count.start()
     load.wait()
     blank = jnp.zeros((32 - members, LANES), F32)
+    half, step = span // n_mem // 2, 8 * LANES
+
+    def fold_rows(index, carry):
+        group, at = index // (half // step), lax.rem(index, half // step) * step
+        ends = []
+        for side in range(2):
+            columns = pl.ds(pl.multiple_of((group * 2 + side) * half + at, LANES), step)
+            ends.append(ens_v[FULL:, columns])
+        tails_ref[group, :, pl.ds(pl.multiple_of(at, LANES), step)] = jnp.concatenate(ends, axis=0)
+        return carry
+
+    lax.fori_loop(0, n_mem * (half // step), fold_rows, 0)
 
     def turn(step, carry):
         for group in range(4):
@@ -191,17 +206,21 @@
             total = jnp.where(quarter == piece, raw[32 * piece:32 * piece + 24, :], total)
         total = jnp.where(ids >= 0, total, 0.0) * w_v[pl.ds(row, 1), :]
         total = jnp.where(sub == members, ids.astype(F32), total)
-        g_ref[row] = jnp.where(sub == members + 1, place.astype(F32), total)
-
-
-def pick(ensemble, ray_cells, ray_weights, n_var):
+        total = jnp.where(sub == members + 1, place.astype(F32), total)
+        g_ref[row] = jnp.where(sub == members + 2, n_v[pl.ds(row, 1), :].astype(F32), total)
+
+
+def pick(ensemble, ray_cells, ray_weights, n_var, n_mem):
     members, span = ensemble.shape
     vmem = pl.BlockSpec(memory_space=pltpu.VMEM)
     return pl.pallas_call(
-        functools.partial(pick_kernel, n_var),
-        out_shape=jax.ShapeDtypeStruct((n_var, 24, LANES), F32),
+        functools.partial(pick_kernel, n_var, n_mem),
+        out_shape=(
+            jax.ShapeDtypeStruct((n_var, 24, LANES), F32),
+            jax.ShapeDtypeStruct((n_mem, 2 * (members - FULL), span // n_mem // 2), F32),
+        ),
         in_specs=[vmem, vmem, pl.BlockSpec(memory_space=pl.ANY)],
-        out_specs=vmem,
+        out_specs=(vmem, vmem),
         scratch_shapes=[
             pltpu.VMEM(ray_cells.shape, jnp.int32),
             pltpu.VMEM(ray_cells.shape, F32),
@@ -241,9 +260,9 @@
     return total + jnp.dot(a_high, b_high, preferred_element_type=F32)
 
 
-def main_kernel(dims, ens_ref, g_ref, centers_ref, obs_ref, var_ref, early_refs, out_ref,
-                par_ref, xf, res, xr, state, xb, agb, inc_v, reg_v, dpoly, dhi, dlo,
-                mini_s, mini_r, fwd_s, fwd_r, own_sem, red_s, red_r, back_s, back_r):
+def main_kernel(dims, ens_ref, tails_ref, g_ref, centers_ref, obs_ref, var_ref, early_refs, out_ref, full_ref,
+                par_ref, xf, xtail, res, rtail, out_v, otail, xr, state, xb, agb, inc_v, reg_v, dpoly, dhi, dlo,
+                mini_s, mini_r, fwd_s, fwd_r, tail_s, tail_r, own_sem, red_s, red_r, back_s, back_r, store_s):
     n_var, n_mem, members, cells, nobs, n_chunk = dims
     group = members // n_mem
     wide = 24 * n_mem
@@ -309,7 +328,7 @@
     def forward(k, chunk):
         there = lax.rem(q + k, n_mem)
         return pltpu.make_async_remote_copy(
-            src_ref=ens_ref.at[:, pl.ds(pl.multiple_of(there * cells + chunk * width, LANES), width)],
+            src_ref=ens_ref.at[pl.ds(0, FULL), pl.ds(pl.multiple_of(there * cells + chunk * width, LANES), width)],
             dst_ref=xf.at[q, :, pl.ds(pl.multiple_of(chunk * width, LANES), width)],
             send_sem=fwd_s.at[k, chunk], recv_sem=fwd_r.at[k, chunk],
             device_id=mem_peer(k), device_id_type=MESH)
@@ -319,21 +338,37 @@
             forward(k, chunk).start()
         return carry
 
-    paced = [EARLY]
+    def forward_tail(k, part):
+        columns = pl.ds(part * (cells // 2 // TAIL_PARTS), cells // 2 // TAIL_PARTS)
+        return pltpu.make_async_remote_copy(
+            src_ref=tails_ref.at[lax.rem(q + k, n_mem), :, columns], dst_ref=xtail.at[q, :, columns],
+            send_sem=tail_s.at[k, part], recv_sem=tail_r.at[k, part],
+            device_id=mem_peer(k), device_id_type=MESH)
+
+    paced = [EARLY - TAIL_PARTS]
 
     def pace(count):
+        while count > 0 and paced[0] < EARLY:
+            for k in (2, 1, 3):
+                forward_tail(k, paced[0] - EARLY + TAIL_PARTS).start()
+            paced[0] += 1
+            count -= 1
         until = min(paced[0] + count, n_chunk)
-        lax.fori_loop(paced[0], until, start_forward, 0)
-        paced[0] = until
+        if until > paced[0]:
+            lax.fori_loop(paced[0], until, start_forward, 0)
+            paced[0] = until
 
     pace(PACE[0])
-    own = pltpu.make_async_copy(ens_ref.at[:, pl.ds(pl.multiple_of(q * cells, LANES), cells)], xf.at[q], own_sem.at[0])
-    own.start()
-    landing = []
+    mine = pl.ds(pl.multiple_of(q * cells, LANES), cells)
+    landing = [
+        pltpu.make_async_copy(ens_ref.at[pl.ds(0, FULL), mine], xf.at[q], own_sem.at[0]),
+        pltpu.make_async_copy(tails_ref.at[q], xtail.at[q], own_sem.at[1]),
+    ]
     for k in range(1, n_mem):
         there = xf.at[lax.rem(q + n_mem - k, n_mem), :, pl.ds(0, EARLY * width)]
         landing.append(pltpu.make_async_copy(early_refs[k - 1], there, own_sem.at[1 + k]))
-        landing[-1].start()
+    for copy in landing:
+        copy.start()
 
     def wait_mini(count):
         landed = g_ref.at[pl.ds(0, count)]
@@ -351,11 +386,13 @@
 
     sub = lax.broadcasted_iota(jnp.int32, (24, LANES), 0)
     ids, places = [], []
+    most = jnp.zeros((1, LANES), F32)
     for source in range(sources):
         for part in range(n_mem):
             tile = xr[part, source]
             state[pl.ds(part * 24, 24), pl.ds(source * LANES, LANES)] = jnp.where(sub < group, tile, 0.0)
         ids.append(xr[0, source, group:group + 1, :])
+        most = jnp.maximum(most, xr[0, source, group + 2:group + 3, :])
         places.append(xr[0, source, group + 1:group + 2, :] + ((first + source) * (n_mem * cells)).astype(F32))
     id_row = jnp.concatenate(ids, axis=1)
     scale = 1.0 / (LRAD * cells)
@@ -381,7 +418,8 @@
         total = jnp.zeros((rays_here, wide), F32)
         for piece in (low, middle, high):
             total = total + lax.dot_general(chosen, piece, (((1,), (1,)), ((), ())), preferred_element_type=F32)
-        xb[batch, q] = jnp.concatenate([total, jnp.zeros((rays_here, LANES - wide), F32)], axis=1)
+        over = jnp.broadcast_to((most > LANES).astype(F32), (rays_here, LANES))
+        xb[batch, q] = jnp.concatenate([total, over[:, wide:]], axis=1)
         for k in (2, 1, 3):
             across(batch, k).start()
 
@@ -409,7 +447,7 @@
         prior = agb[batch]
         obs = par_ref[:, NBATCH + batch:NBATCH + batch + 1]
         error_var = par_ref[:, 2 * NBATCH + batch:2 * NBATCH + batch + 1]
-        mean = jnp.sum(prior, axis=1, keepdims=True) / members
+        mean = jnp.sum(jnp.where(real_lane, prior, 0.0), axis=1, keepdims=True) / members
         anomaly = jnp.where(real_lane, prior - mean, 0.0)
         variance = jnp.sum(anomaly * anomaly, axis=1, keepdims=True) / (members - 1) + EPSILON
         total_var = variance + error_var
@@ -473,63 +511,99 @@
             dhi[half, pl.ds(k * wide, wide), :] = high
             dlo[half, pl.ds(k * wide, wide), :] = low
 
-    own.wait()
+    full_ref[...] = jnp.max(agb[0], axis=0, keepdims=True)
     for copy in landing:
         copy.wait()
-
-    def back(k, chunk):
+    for k in (2, 1, 3):
+        for part in range(TAIL_PARTS):
+            forward_tail(k, part).wait()
+
+    pairs = n_chunk // 2
+    rest = group - FULL
+
+    def columns_of(block_index, pair, side):
+        return pl.ds(pl.multiple_of(block_index * cells + (side * pairs + pair) * width, LANES), width)
+
+    def back(k, pair):
         there = lax.rem(q + k, n_mem)
-        return pltpu.make_async_remote_copy(
-            src_ref=res.at[there, :, pl.ds(pl.multiple_of(chunk * width, LANES), width)],
-            dst_ref=out_ref.at[:, pl.ds(pl.multiple_of(q * cells + chunk * width, LANES), width)],
-            send_sem=back_s.at[k], recv_sem=back_r.at[k],
-            device_id=mem_peer(k), device_id_type=MESH)
+        tail = pl.ds(pl.multiple_of(pair * width, LANES), width)
+        ends = [(res.at[there, :, columns_of(0, pair, side)], out_v.at[pl.ds(0, FULL), columns_of(q, pair, side)])
+                for side in range(2)]
+        ends.append((rtail.at[there, :, tail], otail.at[q, :, tail]))
+        if k == 0:
+            return [pltpu.make_async_copy(a, b, back_r.at[0, pair, n]) for n, (a, b) in enumerate(ends)]
+        return [pltpu.make_async_remote_copy(
+            src_ref=a, dst_ref=b, send_sem=back_s.at[k, pair, n], recv_sem=back_r.at[k, pair, n],
+            device_id=mem_peer(k), device_id_type=MESH) for n, (a, b) in enumerate(ends)]
+
+    def store(source, pair, side):
+        columns = columns_of(source, pair, side)
+        return pltpu.make_async_copy(out_v.at[:, columns], out_ref.at[:, columns], store_s.at[source])
+
+    def drain(pair):
+        tail = pl.ds(pl.multiple_of(pair * width, LANES), width)
+        for k in (0, 1, 3, 2):
+            source = lax.rem(q + n_mem - k, n_mem)
+            for copy in back(k, pair):
+                copy.wait()
+            folded = otail[source, :, tail]
+            for side in range(2):
+                out_v[FULL:, columns_of(source, pair, side)] = folded[side * rest:(side + 1) * rest]
+                store(source, pair, side).start()
 
     pad = jnp.zeros((24 - group, width), F32)
 
-    def apply(chunk, carry):
-        @pl.when(chunk >= EARLY)
+    def apply(pair, carry):
+        tail = pl.ds(pl.multiple_of(pair * width, LANES), width)
+        for side in range(2):
+            chunk = side * pairs + pair
+
+            @pl.when(chunk >= EARLY)
+            def _():
+                for k in (2, 1, 3):
+                    forward(k, chunk).wait()
+
+            at = pl.ds(pl.multiple_of(chunk * width, LANES), width)
+            pieces = []
+            for i in range(n_mem):
+                pieces += [xf[i, :, at], xtail[i, side * rest:(side + 1) * rest, tail], pad]
+            x = jnp.concatenate(pieces, axis=0)
+            high, low = split(x)
+            big, small = dhi[side], dlo[side]
+            y = jnp.dot(big, high, preferred_element_type=F32)
+            y = y + jnp.dot(big, low, preferred_element_type=F32)
+            y = y + jnp.dot(small, high, preferred_element_type=F32)
+            t = (lanes_of((1, width)) + pair * width).astype(F32) * (2.0 / cells)
+            total = y[(terms - 1) * wide:]
+            for k in range(terms - 2, -1, -1):
+                total = y[k * wide:(k + 1) * wide] + t * total
+            total = x + total
+            for i in range(n_mem):
+                res[i, :, at] = total[24 * i:24 * i + FULL]
+                rtail[i, side * rest:(side + 1) * rest, tail] = total[24 * i + FULL:24 * i + group]
+        for k in (2, 1, 3, 0):
+            for copy in back(k, pair):
+                copy.start()
+
+        @pl.when(pair >= LAG)
         def _():
-            for k in (2, 1, 3):
-                forward(k, chunk).wait()
-
-        half = chunk // (n_chunk // 2)
-        at = pl.ds(pl.multiple_of(chunk * width, LANES), width)
-        pieces = []
-        for i in range(n_mem):
-            pieces += [xf[i, :, at], pad]
-        x = jnp.concatenate(pieces, axis=0)
-        high, low = split(x)
-        big, small = dhi[half], dlo[half]
-        y = jnp.dot(big, high, preferred_element_type=F32)
-        y = y + jnp.dot(big, low, preferred_element_type=F32)
-        y = y + jnp.dot(small, high, preferred_element_type=F32)
-        t = (lanes_of((1, width)) + (chunk - half * (n_chunk // 2)) * width).astype(F32) * (2.0 / cells)
-        total = y[(terms - 1) * wide:]
-        for k in range(terms - 2, -1, -1):
-            total = y[k * wide:(k + 1) * wide] + t * total
-        total = x + total
-        for i in range(n_mem):
-            res[i, :, at] = total[24 * i:24 * i + group]
-        for k in (2, 1, 3):
-            back(k, chunk).start()
-        home = pl.ds(pl.multiple_of(q * cells + chunk * width, LANES), width)
-        pltpu.make_async_copy(res.at[q, :, at], out_ref.at[:, home], own_sem.at[1]).start()
-        return carry
-
-    lax.fori_loop(0, n_chunk, apply, 0)
-    mine = pl.ds(pl.multiple_of(q * cells, LANES), cells)
-    keep = pltpu.make_async_copy(res.at[q], out_ref.at[:, mine], own_sem.at[1])
-    for k in range(1, n_mem):
-        source = lax.rem(q + n_mem - k, n_mem)
-        landed = out_ref.at[:, pl.ds(pl.multiple_of(source * cells, LANES), cells)]
-        pltpu.make_async_remote_copy(
-            src_ref=res.at[lax.rem(q + k, n_mem)], dst_ref=landed, send_sem=back_s.at[k], recv_sem=back_r.at[k],
-            device_id=mem_peer(k), device_id_type=MESH).wait()
-    keep.wait()
-
-
-def assimilate(ensemble, picked, ray_centers, obs_values, obs_var, early, n_var, n_mem):
+            drain(pair - LAG)
+
+        return carry
+
+    lax.fori_loop(0, pairs, apply, 0)
+
+    def drain_rest(pair, carry):
+        drain(pair)
+        return carry
+
+    lax.fori_loop(pairs - LAG, pairs, drain_rest, 0)
+    for source in range(n_mem):
+        columns = pl.ds(source * cells, cells)
+        pltpu.make_async_copy(out_v.at[:, columns], out_ref.at[:, columns], store_s.at[source]).wait()
+
+
+def assimilate(ensemble, tails, picked, ray_centers, obs_values, obs_var, early, n_var, n_mem):
     group, span = ensemble.shape
     cells = span // n_mem
     nobs = ray_centers.shape[1]
@@ -542,13 +616,17 @@
     dims = (n_var, n_mem, group * n_mem, cells, nobs, N_CHUNK)
     return pl.pallas_call(
         functools.partial(main_kernel, dims),
-        out_shape=jax.ShapeDtypeStruct((group, span), F32),
-        in_specs=[anywhere, vmem, vmem, vmem, vmem, [anywhere] * len(early)],
-        out_specs=anywhere,
+        out_shape=(jax.ShapeDtypeStruct((group, span), F32), jax.ShapeDtypeStruct((1, LANES), F32)),
+        in_specs=[anywhere, anywhere, vmem, vmem, vmem, vmem, [anywhere] * len(early)],
+        out_specs=(anywhere, vmem),
         scratch_shapes=[
             pltpu.VMEM((nobs, LANES), F32),
-            pltpu.VMEM((n_mem, group, cells), F32),
-            pltpu.VMEM((n_mem, group, cells), F32),
+            pltpu.VMEM((n_mem, FULL, cells), F32),
+            pltpu.VMEM(tails.shape, F32),
+            pltpu.VMEM((n_mem, FULL, cells), F32),
+            pltpu.VMEM(tails.shape, F32),
+            pltpu.VMEM((group, span), F32),
+            pltpu.VMEM(tails.shape, F32),
             pltpu.VMEM((n_mem, n_var // n_mem, 24, LANES), F32),
             pltpu.VMEM((wide, slots), F32),
             pltpu.VMEM((NBATCH, n_mem, rays_here, LANES), F32),
@@ -560,13 +638,15 @@
             pltpu.VMEM((2, (NBATCH + 1) * wide, wide), BF16),
             dma, dma,
             dma((n_mem, N_CHUNK)), dma((n_mem, N_CHUNK)),
+            dma((n_mem, TAIL_PARTS)), dma((n_mem, TAIL_PARTS)),
             dma((1 + n_mem,)),
             dma((NBATCH, n_mem + 1)), dma((NBATCH, n_mem + 1)),
-            dma((n_mem,)), dma((n_mem,)),
+            dma((n_mem, N_CHUNK // 2, 3)), dma((n_mem, N_CHUNK // 2, 3)),
+            dma((n_mem,)),
         ],
         compiler_params=pltpu.CompilerParams(collective_id=1, has_side_effects=True, vmem_limit_bytes=48 << 20),
         name="assimilate",
-    )(ensemble, picked, ray_centers, obs_values, obs_var, early)
+    )(ensemble, tails, picked, ray_centers, obs_values, obs_var, early)
 
 
 def first_columns(ensemble, n_mem):
@@ -576,7 +656,7 @@
     arrived = []
     for k in range(1, n_mem):
         start = lax.rem(q + k, n_mem) * cells
-        piece = lax.dynamic_slice(ensemble, (0, start), (group, EARLY * (cells // N_CHUNK)))
+        piece = lax.dynamic_slice(ensemble, (0, start), (FULL, EARLY * (cells // N_CHUNK)))
         arrived.append(lax.ppermute(piece, "mem", [(i, (i + k) % n_mem) for i in range(n_mem)]))
     return arrived
 
@@ -584,20 +664,13 @@
 def fast(ensemble, ray_cells, ray_weights, ray_centers, obs_values, obs_var):
     n_var, n_mem = lax.axis_size("var"), lax.axis_size("mem")
     early = first_columns(ensemble, n_mem)
-    picked = pick(ensemble, ray_cells, ray_weights, n_var)
-    return assimilate(ensemble, picked, ray_centers, obs_values, obs_var, early, n_var, n_mem)
-
-
-def fits(ray_cells, span, n_var):
-    home = ray_cells.transpose(0, 2, 1) // span
-    hits = home[:, :, None, :] == jnp.arange(n_var, dtype=jnp.int32)[:, None]
-    by_ray = jnp.sum(hits.astype(jnp.int32), axis=(0, 1))
-    return jnp.max(jnp.sum(by_ray.reshape(n_var, n_var, -1), axis=2)) <= LANES
+    picked, tails = pick(ensemble, ray_cells, ray_weights, n_var, n_mem)
+    return assimilate(ensemble, tails, picked, ray_centers, obs_values, obs_var, early, n_var, n_mem)
 
 
 def shards(*arrays):
-    room = fits(arrays[1], arrays[0].shape[1], lax.axis_size("var"))
-    return lax.cond(room, lambda made, *rest: made, lambda made, *rest: plain(*rest), fast(*arrays), *arrays)
+    made, full = fast(*arrays)
+    return lax.cond(full[0, LANES - 1] < 0.5, lambda made, *rest: made, lambda made, *rest: plain(*rest), made, *arrays)
 
 
 def solution(mesh):

time: 180 us -> 164 us (0.911)
  Pallas kernels: 158 us -> 151 us
  other arithmetic: 3.71 us -> 0 us
  waiting for transfers between devices: 3.28 us -> 0.01 us
    pallas_call x2, Pallas kernels: 158 us -> 151 us  [the longest x1 131 us: assimilate(): pl.pallas_call(functools.partial(main_kernel, dims), out_shape=(jax.Shape...]
    ppermute x3, waiting for transfers between devices: 3.28 us -> 0.01 us  [first_columns(): lax.ppermute(piece, 'mem', [(i, (i + k) % n_mem) for i in range(n_mem)])]
    reduce_sum x2 -> x0, other arithmetic: 1.98 us -> none  [the longest x1 1.04 us: fits(): by_ray = jnp.sum(hits.astype(jnp.int32), axis=(0, 1))]
  transfers between devices with their start and end apart: 3 -> 3, of which waited for: 1 -> 0; matrix products, arithmetic and copies ran while one was open for 2% -> 0% of each run, Pallas kernels for 11% -> 12%
where the time goes in v4:
time: 164 us
  Pallas kernels  151 us (92%)
  local copies, waits for them, and re-layouts  7.82 us (5%)
  starting transfers between devices  4.5 us (3%)
    pallas_call x1, Pallas kernels, assimilate(): pl.pallas_call(functools.partial(main_kernel, dims), out_shape=(jax.Shape...  131 us
    pallas_call x1, Pallas kernels, pick(): pl.pallas_call(functools.partial(pick_kernel, n_var, n_mem), out_shape=(j...  20 us
    unnamed x11, local copies, waits for them, and re-layouts  5.92 us
    ppermute x3, starting transfers between devices, first_columns(): lax.ppermute(piece, 'mem', [(i, (i + k) % n_mem) for i in range(n_mem)])  4.5 us
  transfers between devices with their start and end apart: 3, of which 0 were waited for; matrix products, arithmetic and copies ran while one was open for 0% of the time, Pallas kernels for 12%

profile of v4, /device:TPU:1, one launch (start us, length us, event | category | flops | bytes accessed | tf_op | source)
XLA Modules:
  0.0 164.1 jit_solution(16813427343171707582)
XLA Ops:
  0.0 0.0 copy-start.4
  0.0 0.0 copy-start.3
  0.0 0.0 copy-start.2
  0.0 1.3 constant_dynamic-slice_fusion
  1.4 0.0 copy-start
  1.4 0.0 copy-start.1
  1.4 3.4 %collective-permute-start.2 = (f32[16,6144]{1,0:T(8,128)S(1)}, f32[16,6144]{1,0:T(8,128)S(1)}, u32[]{:S(2)}, u32[]{:S(2)}) collective-permute-start(f32[16,6144]{1,0:T(8,128)S(1)} %get-tuple-element.95), channel_id=1, source_target_pairs={{0,3},{1,0},{2,1},{3,2},{4,7},{5,4},{6,5},{7,6},{8,11},{9,8},{10,9... | collective-permute-start | bytes 1179656 | tf_op jit(solution)/shard_map/ppermute | solution.py:660
  4.8 0.5 collective-permute-start.1
  5.3 0.6 collective-permute-start
  5.9 20.0 %pick.1 = (f32[32,24,128]{2,1,0:T(8,128)S(1)}, f32[4,8,8192]{2,1,0:T(8,128)S(1)}) custom-call(s32[4,64,256]{2,1,0:T(8,128)} %bitcast.156, f32[4,64,256]{2,1,0:T(8,128)} %bitcast.157, f32[20,65536]{1,0:T(8,128)} %ens_ref.3), custom_call_target="tpu_custom_call" | custom-call | flops 1073741824 | bytes 67108864 | tf_op jit(solution)/shard_map/pick/pallas_call | solution.py:216
  25.9 0.0 collective-permute-done.2.early_refs_2_
  25.9 0.0 collective-permute-done.1.early_refs_1_
  25.9 0.0 collective-permute-done.early_refs_0_
  25.9 0.0 copy-done.4
  25.9 0.0 copy-done.3
  25.9 0.0 copy-done.2
  25.9 130.8 %assimilate.1 = (f32[20,65536]{1,0:T(8,128)}, f32[1,128]{1,0:T(1,128)S(1)}) custom-call(f32[20,65536]{1,0:T(8,128)} %ens_ref.3, f32[4,8,8192]{2,1,0:T(8,128)S(1)} %get-tuple-element.32.tails_ref, f32[32,24,128]{2,1,0:T(8,128)S(1)} %get-tuple-element.33.g_ref, s32[4,256]{1,0:T(4,128)S(1)} %copy-done.2, f32[4,256]{1,0:T(4,128)S(1)} %copy-done.3, ...), custom_call_target="tpu_custom_call" | custom-call | tf_op jit(solution)/shard_map/assimilate/pallas_call | solution.py:617
  156.7 0.6 slice.63
  158.0 0.0 copy-done
  158.0 0.0 copy-done.1
  158.0 0.2 conditional.1
  158.2 5.9 %copy.68 = f32[20,65536]{1,0:T(8,128)} copy(f32[20,65536]{1,0:T(8,128)} %get-tuple-element.36) | data formatting | bytes 10485760
Async XLA Ops:
  0.0 25.9 %copy-start.4 = (f32[4,256]{1,0:T(4,128)S(1)}, f32[4,256]{1,0:T(4,128)}, u32[]{:S(2)}) copy-start(f32[4,256]{1,0:T(4,128)} %var_ref.1) | copy-start | bytes 12292
  0.0 25.9 %copy-start.3 = (f32[4,256]{1,0:T(4,128)S(1)}, f32[4,256]{1,0:T(4,128)}, u32[]{:S(2)}) copy-start(f32[4,256]{1,0:T(4,128)} %obs_ref.1) | copy-start | bytes 12292
  0.0 25.9 %copy-start.2 = (s32[4,256]{1,0:T(4,128)S(1)}, s32[4,256]{1,0:T(4,128)}, u32[]{:S(2)}) copy-start(s32[4,256]{1,0:T(4,128)} %centers_ref.1) | copy-start | bytes 12292
  1.4 156.6 %copy-start = (s32[4,256,64]{1,2,0:T(8,128)S(1)}, s32[4,256,64]{1,2,0:T(8,128)}, u32[]{:S(2)}) copy-start(s32[4,256,64]{1,2,0:T(8,128)} %param.11) | copy-start | bytes 786436
  1.4 156.6 %copy-start.1 = (f32[4,256,64]{1,2,0:T(8,128)S(1)}, f32[4,256,64]{1,2,0:T(8,128)}, u32[]{:S(2)}) copy-start(f32[4,256,64]{1,2,0:T(8,128)} %param.12) | copy-start | bytes 786436
  1.4 24.5 %collective-permute-start.2 = (f32[16,6144]{1,0:T(8,128)S(1)}, f32[16,6144]{1,0:T(8,128)S(1)}, u32[]{:S(2)}, u32[]{:S(2)}) collective-permute-start(f32[16,6144]{1,0:T(8,128)S(1)} %get-tuple-element.95), channel_id=1, source_target_pairs={{0,3},{1,0},{2,1},{3,2},{4,7},{5,4},{6,5},{7,6},{8,11},{9,8},{10,9... | collective-permute-start | bytes 1179656 | tf_op jit(solution)/shard_map/ppermute | solution.py:660
  4.8 21.1 %collective-permute-start.1 = (f32[16,6144]{1,0:T(8,128)S(1)}, f32[16,6144]{1,0:T(8,128)S(1)}, u32[]{:S(2)}, u32[]{:S(2)}) collective-permute-start(f32[16,6144]{1,0:T(8,128)S(1)} %get-tuple-element.96), channel_id=1, source_target_pairs={{0,2},{1,3},{2,0},{3,1},{4,6},{5,7},{6,4},{7,5},{8,10},{9,11},{10,... | collective-permute-start | bytes 1179656 | tf_op jit(solution)/shard_map/ppermute | solution.py:660
  5.3 20.6 %collective-permute-start = (f32[16,6144]{1,0:T(8,128)S(1)}, f32[16,6144]{1,0:T(8,128)S(1)}, u32[]{:S(2)}, u32[]{:S(2)}) collective-permute-start(f32[16,6144]{1,0:T(8,128)S(1)} %get-tuple-element.97), channel_id=1, source_target_pairs={{0,1},{1,2},{2,3},{3,0},{4,5},{5,6},{6,7},{7,4},{8,9},{9,10},{10,1... | collective-permute-start | bytes 1179656 | tf_op jit(solution)/shard_map/ppermute | solution.py:660

commit v5 on v4

--- a/solution.py
+++ b/solution.py
@@ -243,10 +243,6 @@
     )(ray_cells.transpose(0, 2, 1), ray_weights.transpose(0, 2, 1), ensemble)
 
 
-def high_dot(a, b):
-    return jnp.dot(a, b, precision=HIGHEST_PREC, preferred_element_type=F32)
-
-
 def split(x):
     high = x.astype(BF16)
     return high, (x - high.astype(F32)).astype(BF16)
@@ -410,13 +406,9 @@
 
     def start_reduce(batch):
         chosen = (id_row == own_ray + batch * rays_here).astype(BF16)
-        held = state[...]
-        high = held.astype(BF16)
-        rest = held - high.astype(F32)
-        middle = rest.astype(BF16)
-        low = (rest - middle.astype(F32)).astype(BF16)
+        high, low = split(state[...])
         total = jnp.zeros((rays_here, wide), F32)
-        for piece in (low, middle, high):
+        for piece in (low, high):
             total = total + lax.dot_general(chosen, piece, (((1,), (1,)), ((), ())), preferred_element_type=F32)
         over = jnp.broadcast_to((most > LANES).astype(F32), (rays_here, LANES))
         xb[batch, q] = jnp.concatenate([total, over[:, wide:]], axis=1)
@@ -474,14 +466,14 @@
             beta = jnp.where(inside, far - near, 0.0)
             regress = reg_v[...]
             both = jnp.concatenate([regress * alpha, regress * beta], axis=1)
-            ab = high_dot(inc_v[0:wide, :], both)
+            ab = split_dot(inc_v[0:wide, :], both)
             a, b = ab[:, :LANES], ab[:, LANES:]
             if batch == 0:
                 dpoly[half, 0], dpoly[half, 1] = a, b
                 continue
             old = jnp.concatenate([dpoly[half, k] for k in range(batch + 1)], axis=1)
             left = jnp.concatenate([a[:, 0:wide], b[:, 0:wide]], axis=0)
-            made = high_dot(left, old)
+            made = split_dot(left, old)
             for k in range(batch + 2):
                 total = a if k == 0 else b if k == 1 else jnp.zeros_like(a)
                 if k <= batch:

time: 164 us -> 163 us (level)
  Pallas kernels: 151 us -> 149 us
where the time goes in v5:
time: 163 us
  Pallas kernels  149 us (91%)
  local copies, waits for them, and re-layouts  7.82 us (5%)
  starting transfers between devices  4.5 us (3%)
    pallas_call x1, Pallas kernels, assimilate(): pl.pallas_call(functools.partial(main_kernel, dims), out_shape=(jax.Shape...  129 us
    pallas_call x1, Pallas kernels, pick(): pl.pallas_call(functools.partial(pick_kernel, n_var, n_mem), out_shape=(j...  20 us
    unnamed x11, local copies, waits for them, and re-layouts  5.92 us
    ppermute x3, starting transfers between devices, first_columns(): lax.ppermute(piece, 'mem', [(i, (i + k) % n_mem) for i in range(n_mem)])  4.5 us
  transfers between devices with their start and end apart: 3, of which 0 were waited for; matrix products, arithmetic and copies ran while one was open for 0% of the time, Pallas kernels for 12%

profile of v5, /device:TPU:1, one launch (start us, length us, event | category | flops | bytes accessed | tf_op | source)
XLA Modules:
  0.0 162.7 jit_solution(11483480987101921383)
XLA Ops:
  0.0 0.0 copy-start.4
  0.0 0.0 copy-start.3
  0.0 0.0 copy-start.2
  0.0 1.3 constant_dynamic-slice_fusion
  1.4 0.0 copy-start
  1.4 0.0 copy-start.1
  1.4 3.4 %collective-permute-start.2 = (f32[16,6144]{1,0:T(8,128)S(1)}, f32[16,6144]{1,0:T(8,128)S(1)}, u32[]{:S(2)}, u32[]{:S(2)}) collective-permute-start(f32[16,6144]{1,0:T(8,128)S(1)} %get-tuple-element.95), channel_id=1, source_target_pairs={{0,3},{1,0},{2,1},{3,2},{4,7},{5,4},{6,5},{7,6},{8,11},{9,8},{10,9... | collective-permute-start | bytes 1179656 | tf_op jit(solution)/shard_map/ppermute | solution.py:652
  4.8 0.5 collective-permute-start.1
  5.3 0.6 collective-permute-start
  5.9 20.0 %pick.1 = (f32[32,24,128]{2,1,0:T(8,128)S(1)}, f32[4,8,8192]{2,1,0:T(8,128)S(1)}) custom-call(s32[4,64,256]{2,1,0:T(8,128)} %bitcast.156, f32[4,64,256]{2,1,0:T(8,128)} %bitcast.157, f32[20,65536]{1,0:T(8,128)} %ens_ref.3), custom_call_target="tpu_custom_call" | custom-call | flops 1073741824 | bytes 67108864 | tf_op jit(solution)/shard_map/pick/pallas_call | solution.py:216
  25.9 0.0 collective-permute-done.2.early_refs_2_
  25.9 0.0 collective-permute-done.1.early_refs_1_
  26.0 0.0 collective-permute-done.early_refs_0_
  26.0 0.0 copy-done.4
  26.0 0.0 copy-done.3
  26.0 0.0 copy-done.2
  26.0 129.3 %assimilate.1 = (f32[20,65536]{1,0:T(8,128)}, f32[1,128]{1,0:T(1,128)S(1)}) custom-call(f32[20,65536]{1,0:T(8,128)} %ens_ref.3, f32[4,8,8192]{2,1,0:T(8,128)S(1)} %get-tuple-element.32.tails_ref, f32[32,24,128]{2,1,0:T(8,128)S(1)} %get-tuple-element.33.g_ref, s32[4,256]{1,0:T(4,128)S(1)} %copy-done.2, f32[4,256]{1,0:T(4,128)S(1)} %copy-done.3, ...), custom_call_target="tpu_custom_call" | custom-call | tf_op jit(solution)/shard_map/assimilate/pallas_call | solution.py:609
  155.3 0.6 slice.63
  156.5 0.0 copy-done
  156.5 0.0 copy-done.1
  156.5 0.3 conditional.1
  156.8 5.9 %copy.68 = f32[20,65536]{1,0:T(8,128)} copy(f32[20,65536]{1,0:T(8,128)} %get-tuple-element.36) | data formatting | bytes 10485760
Async XLA Ops:
  0.0 26.0 %copy-start.4 = (f32[4,256]{1,0:T(4,128)S(1)}, f32[4,256]{1,0:T(4,128)}, u32[]{:S(2)}) copy-start(f32[4,256]{1,0:T(4,128)} %var_ref.1) | copy-start | bytes 12292
  0.0 26.0 %copy-start.3 = (f32[4,256]{1,0:T(4,128)S(1)}, f32[4,256]{1,0:T(4,128)}, u32[]{:S(2)}) copy-start(f32[4,256]{1,0:T(4,128)} %obs_ref.1) | copy-start | bytes 12292
  0.0 26.0 %copy-start.2 = (s32[4,256]{1,0:T(4,128)S(1)}, s32[4,256]{1,0:T(4,128)}, u32[]{:S(2)}) copy-start(s32[4,256]{1,0:T(4,128)} %centers_ref.1) | copy-start | bytes 12292
  1.4 155.1 %copy-start = (s32[4,256,64]{1,2,0:T(8,128)S(1)}, s32[4,256,64]{1,2,0:T(8,128)}, u32[]{:S(2)}) copy-start(s32[4,256,64]{1,2,0:T(8,128)} %param.11) | copy-start | bytes 786436
  1.4 155.1 %copy-start.1 = (f32[4,256,64]{1,2,0:T(8,128)S(1)}, f32[4,256,64]{1,2,0:T(8,128)}, u32[]{:S(2)}) copy-start(f32[4,256,64]{1,2,0:T(8,128)} %param.12) | copy-start | bytes 786436
  1.4 24.6 %collective-permute-start.2 = (f32[16,6144]{1,0:T(8,128)S(1)}, f32[16,6144]{1,0:T(8,128)S(1)}, u32[]{:S(2)}, u32[]{:S(2)}) collective-permute-start(f32[16,6144]{1,0:T(8,128)S(1)} %get-tuple-element.95), channel_id=1, source_target_pairs={{0,3},{1,0},{2,1},{3,2},{4,7},{5,4},{6,5},{7,6},{8,11},{9,8},{10,9... | collective-permute-start | bytes 1179656 | tf_op jit(solution)/shard_map/ppermute | solution.py:652
  4.8 21.2 %collective-permute-start.1 = (f32[16,6144]{1,0:T(8,128)S(1)}, f32[16,6144]{1,0:T(8,128)S(1)}, u32[]{:S(2)}, u32[]{:S(2)}) collective-permute-start(f32[16,6144]{1,0:T(8,128)S(1)} %get-tuple-element.96), channel_id=1, source_target_pairs={{0,2},{1,3},{2,0},{3,1},{4,6},{5,7},{6,4},{7,5},{8,10},{9,11},{10,... | collective-permute-start | bytes 1179656 | tf_op jit(solution)/shard_map/ppermute | solution.py:652
  5.3 20.7 %collective-permute-start = (f32[16,6144]{1,0:T(8,128)S(1)}, f32[16,6144]{1,0:T(8,128)S(1)}, u32[]{:S(2)}, u32[]{:S(2)}) collective-permute-start(f32[16,6144]{1,0:T(8,128)S(1)} %get-tuple-element.97), channel_id=1, source_target_pairs={{0,1},{1,2},{2,3},{3,0},{4,5},{5,6},{6,7},{7,4},{8,9},{9,10},{10,1... | collective-permute-start | bytes 1179656 | tf_op jit(solution)/shard_map/ppermute | solution.py:652
